TPU v7x, 128 devices: a whole 4x4x4 slice. The times are simulated.
128 devices in a mesh: seq: 8 (over z, core), chan: 16 (over y, x).
Axes of the slice: x: 4, y: 4, z: 4, core: 2. Of those that a mesh axis runs over, the one named last changes fastest.
Arguments:
- x_in: bfloat16 [2048, 8192], P('seq', 'chan'), may hold values from -6 to 6
- z_in: bfloat16 [2048, 8192], P('seq', 'chan'), may hold values from -6 to 6
- grad_out: bfloat16 [2048, 8192], P('seq', 'chan'), may hold values from -6 to 6
- conv_w: float32 [4, 8192], P(None, 'chan'), may hold values from -3 to 3
- conv_b: float32 [8192], P('chan'), may hold values from -3 to 3
- xproj_w: bfloat16 [8192, 288], P('chan'), may hold values from -0.0625 to 0.0625
- dt_w: bfloat16 [256, 8192], P(None, 'chan'), may hold values from -0.375 to 0.375
- dt_bias: float32 [8192], P('chan'), may hold values from -4 to -3
- a_log: float32 [8192, 16], P('chan'), as said below
- d_skip: float32 [8192], P('chan'), may hold values from 0.5 to 1.5
- dt_gain: float32 [256], replicated, may hold values from 0.1 to 1.9
Outputs:
- x_grad: bfloat16 [2048, 8192], P('seq', 'chan')
- z_grad: bfloat16 [2048, 8192], P('seq', 'chan')
- conv_w_grad: float32 [4, 8192], P(None, 'chan')
- conv_b_grad: float32 [8192], P('chan')
- xproj_grad: float32 [8192, 288], P('chan')
- dt_w_grad: float32 [256, 8192], P(None, 'chan')
- dt_bias_grad: float32 [8192], P('chan')
- a_log_grad: float32 [8192, 16], P('chan')
- d_skip_grad: float32 [8192], P('chan')
- dt_gain_grad: float32 [256], replicated
Inputs may be any that keep to these rules, and one draw needn't show every extreme that they name: rates -exp(a_log) are spread over channels; their mix depends on the seed.
All inputs are finite; a program needn't handle non-finite values.
Results may differ from a plain program's by a relative error of at most 0.025.
Values may be sent and summed in bfloat16 or wider, within the bound.
A program may use at most 192 MiB of HBM per device.

v0:
```python
import functools
import math

import jax
import jax.numpy as jnp
from jax import lax
from jax.experimental import pallas as pl
from jax.experimental.pallas import tpu as pltpu
from jax.sharding import PartitionSpec as P

EPS = 1e-06
LOG2E = 1.4426950408889634
LANES = 128
GROUP = 16
F32 = jnp.float32
BF16 = jnp.bfloat16
MESH = pl.DeviceIdType.MESH


def dot(a, b):
    return jnp.dot(a, b, preferred_element_type=F32)


def dot_nt(a, b):
    return lax.dot_general(a, b, (((1,), (1,)), ((), ())), preferred_element_type=F32)


def iota(shape, dim):
    return lax.broadcasted_iota(jnp.int32, shape, dim)


def silu_grad(value):
    sigma = jax.nn.sigmoid(value)
    return sigma * (1.0 + value * (1.0 - sigma))


def softplus(value):
    return jnp.maximum(value, 0.0) + jnp.log1p(jnp.exp(-jnp.abs(value)))


class Exchange:
    def __init__(self, axis, count, me, send_sem, recv_sem):
        self.axis, self.count, self.me = axis, count, me
        self.send_sem, self.recv_sem = send_sem, recv_sem

    def _copy(self, src, dst, send, recv, peer):
        return pltpu.make_async_remote_copy(
            src_ref=src,
            dst_ref=dst,
            send_sem=self.send_sem.at[send],
            recv_sem=self.recv_sem.at[recv],
            device_id={self.axis: peer},
            device_id_type=MESH,
        )

    def peers(self):
        return [lax.rem(self.me + d, self.count) for d in range(1, self.count)]

    def send(self, src, dst, peer):
        self._copy(src, dst, peer, self.me, peer).start()

    def wait_recv(self, slot, peer):
        self._copy(slot, slot, peer, peer, peer).wait_recv()

    def wait_send(self, slot, peer):
        self._copy(slot, slot, peer, peer, peer).wait_send()


def layer_kernel(dims, *refs):
    T, C, NS, NC, R, N = dims
    (x_ref, z_ref, g_ref, cw_ref, cb_ref, xw_ref, dw_ref, db_ref, al_ref, ds_ref, dg_ref,
     xg_o, zg_o, cwg_o, cbg_o, xpg_o, dwg_o, dbg_o, alg_o, dsg_o, dgg_o,
     xpad, pre_act, u_bf, ut_bf, gy, gz, xwp, part, send1, rs1, ag1, low_own, inv_own,
     pre_soft, delta, drive, bB, cB, a_buf, h_buf, lam_buf, ha_buf,
     st_f, st_b, tot, in_f, in_b, in_tot, carry_f, carry_b,
     e_exp, m_b, m_c, sel_b, sel_c, dmask, back_b, back_c,
     yv, bcg, uscan, pregrad, prehalf, send2, rs2, ag2,
     dw_f, dw_send, dw_rs, dw_ag, xl_f, xl_send, xl_rs, xl_ag, sm_f, sm_rs, sm_ag,
     halo_x, halo_a, apad,
     s_c, r_c, s_st, r_st, s_sq, r_sq, s_h, r_h) = refs
    ROWS = T // NC
    W = R + LANES
    NB = T // GROUP
    GN = GROUP * N
    RB, CB = R // NS, C // NS
    SM = sm_f.shape[0]
    SB = SM // NS
    ms, mc = lax.axis_index("seq"), lax.axis_index("chan")

    def chan(k):
        return Exchange("chan", NC, mc, s_c.at[k], r_c.at[k])

    def seq(k):
        return Exchange("seq", NS, ms, s_sq.at[k], r_sq.at[k])

    def states(k):
        return Exchange("seq", NS, ms, s_st.at[k], r_st.at[k])

    barrier = pltpu.get_barrier_semaphore()
    for d in range(1, NC):
        pl.semaphore_signal(barrier, inc=1, device_id={"chan": lax.rem(mc + d, NC)}, device_id_type=MESH)
    for d in range(1, NS):
        pl.semaphore_signal(barrier, inc=1, device_id={"seq": lax.rem(ms + d, NS)}, device_id_type=MESH)

    e_exp[...] = (iota((GN, GROUP), 0) // N == iota((GN, GROUP), 1)).astype(F32).astype(BF16)
    row_n, lane = iota((GN, LANES), 0) % N, iota((GN, LANES), 1)
    m_b[...] = ((lane == row_n) | (lane == row_n + 2 * N)).astype(F32)
    m_c[...] = ((lane == row_n + N) | (lane == row_n + 3 * N)).astype(F32)
    back_b[...] = (lane == row_n).astype(F32).astype(BF16)
    back_c[...] = (lane == row_n + N).astype(F32).astype(BF16)
    k_row, col_n = iota((LANES, GN), 0), iota((LANES, GN), 1) % N
    sel_b[...] = ((k_row == col_n) | (k_row == col_n + 2 * N)).astype(F32).astype(BF16)
    sel_c[...] = ((k_row == col_n + N) | (k_row == col_n + 3 * N)).astype(F32).astype(BF16)
    dmask[...] = (iota((GROUP, GN), 1) // N == iota((GROUP, GN), 0)).astype(F32)
    xwp[...] = jnp.zeros_like(xwp)
    xwp[:, : R + 2 * N] = xw_ref[...]

    xpad[:8, :] = jnp.zeros((8, C), F32)
    xpad[8:, :] = x_ref[...].astype(F32)
    cw = cw_ref[...]

    def conv(first, count):
        total = jnp.broadcast_to(cb_ref[...], (count, C))
        for k in range(4):
            total = total + cw[k : k + 1] * xpad[first + 5 + k : first + 5 + k + count, :]
        return total

    pre_act[...] = conv(0, T)
    pl.semaphore_wait(barrier, NC + NS - 2)
    halo = Exchange("seq", NS, ms, s_h, r_h)

    def halo_copy(src, dst, k, peer):
        return pltpu.make_async_remote_copy(
            src_ref=src, dst_ref=dst, send_sem=s_h.at[k], recv_sem=r_h.at[k],
            device_id={"seq": peer}, device_id_type=MESH,
        )

    after, before = lax.rem(ms + 1, NS), lax.rem(ms + NS - 1, NS)

    @pl.when(ms < NS - 1)
    def _():
        halo_copy(x_ref.at[T - 16 :, :], halo_x, 0, after).start()

    gate = z_ref[...].astype(F32)
    cot = g_ref[...].astype(F32)
    sig = jax.nn.sigmoid(gate)
    gy[...] = cot * gate * sig
    gz[...] = cot * sig * (1.0 + gate * (1.0 - sig))

    @pl.when(ms > 0)
    def _():
        halo_copy(halo_x, halo_x, 0, before).wait_recv()
        xpad[:8, :] = halo_x[...].astype(F32)[8:16]
        pre_act[:8, :] = conv(0, 8)

    act = pre_act[...]
    u_bf[...] = (act * jax.nn.sigmoid(act)).astype(BF16)

    part[...] = dot(u_bf[...], xwp[...])
    send1[...] = part[...].astype(BF16)

    def my_rows(ref):
        return ref[pl.ds(pl.multiple_of(mc * ROWS, ROWS), ROWS), :]

    def block(ref, i, size):
        return ref.at[pl.ds(pl.multiple_of(i * size, size), size), :]

    def scatter(ex, src, slots, size):
        for peer in ex.peers():
            ex.send(block(src, peer, size), slots.at[ex.me], peer)

    def collect(ex, slots, own):
        for peer in ex.peers():
            ex.wait_recv(slots.at[peer], peer)
        for peer in ex.peers():
            own = own + slots[peer].astype(F32)
        return own

    def spread(ex, buf, size):
        for peer in ex.peers():
            ex.send(block(buf, ex.me, size), block(buf, ex.me, size), peer)

    def arrive(ex, buf, size):
        for peer in ex.peers():
            ex.wait_recv(block(buf, peer, size), peer)

    scatter(chan(0), send1, rs1, ROWS)
    ut_bf[...] = u_bf[...].astype(F32).T.astype(BF16)
    rate = -jnp.exp(al_ref[...].T)
    rate2 = rate * LOG2E
    proj = collect(chan(0), rs1, my_rows(part))
    low = proj[:, :R]
    inv = lax.rsqrt(jnp.mean(low * low, -1, keepdims=True) + EPS)
    low_own[...] = low
    inv_own[...] = jnp.broadcast_to(inv, inv_own.shape)
    tail = proj[:, R:]
    tail_hi = tail.astype(BF16).astype(F32)
    tail = tail_hi + pltpu.roll(tail - tail_hi, 2 * N, 1)
    mine = pl.ds(pl.multiple_of(mc * ROWS, ROWS), ROWS)
    ag1[mine, :R] = (low * inv * dg_ref[...]).astype(BF16)
    ag1[mine, R:] = tail.astype(BF16)
    spread(chan(1), ag1, ROWS)
    arrive(chan(1), ag1, ROWS)

    soft = dot(ag1[:, :R], dw_ref[...]) + db_ref[...]
    pre_soft[...] = soft
    step = softplus(soft)
    delta[...] = step
    drive[...] = step * u_bf[...].astype(F32)
    tot[...] = jnp.sum(step, 0, keepdims=True)
    for peer in states(2).peers():
        states(2).send(tot, in_tot.at[ms], peer)

    ones = jnp.ones((LANES, LANES), BF16)

    def widen(i, carry):
        rows = ag1[pl.ds(pl.multiple_of(i * GROUP, GROUP), GROUP), R:]
        spread_rows = dot(e_exp[...], rows)
        at = pl.ds(pl.multiple_of(i * GN, GN), GN)
        bB[at, :] = dot((spread_rows * m_b[...]).astype(BF16), ones)
        cB[at, :] = dot((spread_rows * m_c[...]).astype(BF16), ones)
        return carry

    lax.fori_loop(0, NB, widen, 0)

    def row(ref, t):
        return ref[pl.ds(t, 1), :]

    def state_at(t):
        return pl.ds(pl.multiple_of(t * N, N), N)

    def wide(ref, t):
        return jnp.concatenate([ref[state_at(t), :]] * (C // LANES), axis=1)

    zero_state = jnp.zeros((N, C), F32)

    def forward_part(i, h):
        for j in range(GROUP):
            t = i * GROUP + j
            a = jnp.exp2(row(delta, t) * rate2)
            a_buf[state_at(t), :] = a
            h = a * h + row(drive, t) * wide(bB, t)
        return h

    st_f[...] = lax.fori_loop(0, NB, forward_part, zero_state).astype(BF16)
    for d in range(1, NS):

        @pl.when(ms + d < NS)
        def _(d=d):
            states(0).send(st_f, in_f.at[ms], ms + d)

    def backward_part(i, g):
        for j in range(GROUP):
            t = T - 1 - (i * GROUP + j)
            g = a_buf[state_at(t), :] * (row(gy, t) * wide(cB, t) + g)
        return g

    st_b[...] = lax.fori_loop(0, NB, backward_part, zero_state).astype(BF16)
    for d in range(1, NS):

        @pl.when(ms - d >= 0)
        def _(d=d):
            states(1).send(st_b, in_b.at[ms], ms - d)

    for peer in states(2).peers():
        states(2).wait_recv(in_tot.at[peer], peer)
    carry_f[...] = zero_state
    for s in range(NS - 1):

        @pl.when(s < ms)
        def _(s=s):
            states(0).wait_recv(in_f.at[s], s)
            carry_f[...] = jnp.exp2(in_tot[s] * rate2) * carry_f[...] + in_f[s].astype(F32)

    start = carry_f[...]
    h_buf[:N, :] = start.astype(BF16)

    def forward(i, h):
        for j in range(GROUP):
            t = i * GROUP + j
            h = a_buf[state_at(t), :] * h + row(drive, t) * wide(bB, t)
            h_buf[state_at(t + 1), :] = h.astype(BF16)
        return h

    lax.fori_loop(0, NB, forward, start)

    def tokens(i):
        return pl.ds(pl.multiple_of(i * GROUP, GROUP), GROUP)

    def after_forward(i, carry):
        coef = ag1[tokens(i), R:]
        h_rows = h_buf[pl.ds(pl.multiple_of(i * GN + N, N), GN), :]
        c_diag = (dot(coef, sel_c[...]) * dmask[...]).astype(BF16)
        yv[tokens(i), :] = dot(c_diag, h_rows)
        c_all = dot_nt(gy[tokens(i), :].astype(BF16), h_rows) * dmask[...]
        bcg[tokens(i), :] = dot(c_all.astype(BF16), back_c[...])
        return carry

    lax.fori_loop(0, NB, after_forward, 0)

    carry_b[...] = zero_state
    for s in range(NS - 1, 0, -1):

        @pl.when(s > ms)
        def _(s=s):
            states(1).wait_recv(in_b.at[s], s)
            carry_b[...] = jnp.exp2(in_tot[s] * rate2) * carry_b[...] + in_b[s].astype(F32)

    def backward(i, carry):
        g, acc = carry
        for j in range(GROUP):
            t = T - 1 - (i * GROUP + j)
            lam = row(gy, t) * wide(cB, t) + g
            g = a_buf[state_at(t), :] * lam
            hold = g * h_buf[state_at(t), :].astype(F32)
            acc = acc + hold * row(delta, t)
            lam_buf[state_at(t), :] = lam.astype(BF16)
            ha_buf[state_at(t), :] = (hold * rate).astype(BF16)
        return g, acc

    _, rate_sum = lax.fori_loop(0, NB, backward, (carry_b[...], zero_state))

    def after_backward(i, carry):
        coef = ag1[tokens(i), R:]
        at = pl.ds(pl.multiple_of(i * GN, GN), GN)
        lam_rows = lam_buf[at, :]
        b_diag = (dot(coef, sel_b[...]) * dmask[...]).astype(BF16)
        adj_b = dot(b_diag, lam_rows)
        by_rate = dot(dmask[...].astype(BF16), ha_buf[at, :])
        b_all = dot_nt(drive[tokens(i), :].astype(BF16), lam_rows) * dmask[...]
        bcg[tokens(i), :] = bcg[tokens(i), :] + dot(b_all.astype(BF16), back_b[...])
        pre = (by_rate + adj_b * u_bf[tokens(i), :].astype(F32)) * jax.nn.sigmoid(pre_soft[tokens(i), :])
        pregrad[tokens(i), :] = pre
        prehalf[tokens(i), :] = pre.astype(BF16)
        uscan[tokens(i), :] = ds_ref[...] * gy[tokens(i), :] + delta[tokens(i), :] * adj_b
        return carry

    lax.fori_loop(0, NB, after_backward, 0)

    part[:, :R] = dot_nt(prehalf[...], dw_ref[...])
    part[:, R:] = bcg[...]
    send2[...] = part[...].astype(BF16)
    scatter(chan(2), send2, rs2, ROWS)

    dw_f[...] = dot(ag1[:, :R].astype(F32).T.astype(BF16), prehalf[...])
    dw_send[...] = dw_f[...].astype(BF16)
    scatter(seq(0), dw_send, dw_rs, RB)
    u32 = u_bf[...].astype(F32)
    zg_o[...] = (gz[...] * (yv[...] + ds_ref[...] * u32)).astype(BF16)
    sm_f[...] = jnp.zeros_like(sm_f)
    sm_f[2 * N : 3 * N, :] = rate_sum * rate
    sm_f[3 * N + 5 : 3 * N + 6, :] = jnp.sum(pregrad[...], 0, keepdims=True)
    sm_f[3 * N + 6 : 3 * N + 7, :] = jnp.sum(gy[...] * u32, 0, keepdims=True)

    grad_rows = collect(chan(2), rs2, my_rows(part))
    low = low_own[...]
    inv = inv_own[:, :1]
    scaled = grad_rows[:, :R] * dg_ref[...]
    low_grad = inv * scaled - low * (inv * inv * inv) * jnp.mean(scaled * low, -1, keepdims=True)
    gain = jnp.sum(grad_rows[:, :R] * low * inv, 0, keepdims=True)
    half = LANES // 2
    lanes = iota((ROWS, LANES), 1)
    rows = iota((ROWS, LANES), 0)
    g0 = jnp.broadcast_to(gain[:, :LANES], (ROWS, LANES))
    g1 = jnp.broadcast_to(gain[:, LANES:], (ROWS, LANES))
    q = rows % 4
    gq = jnp.where(q == 0, pltpu.roll(g0, half, 1), jnp.where(q == 1, g0, jnp.where(q == 2, pltpu.roll(g1, half, 1), g1)))
    g_hi = gq.astype(BF16).astype(F32)
    g_rows = jnp.where(rows < 4, g_hi, jnp.where(rows < 8, gq - g_hi, 0.0))
    ag2[mine, :R] = low_grad.astype(BF16)
    ag2[mine, R:] = jnp.where(lanes < half, grad_rows[:, R:], g_rows).astype(BF16)
    spread(chan(3), ag2, ROWS)

    own = collect(seq(0), dw_rs, dw_f[pl.ds(pl.multiple_of(ms * RB, RB), RB), :])
    dw_ag[pl.ds(pl.multiple_of(ms * RB, RB), RB), :] = own.astype(BF16)
    spread(seq(1), dw_ag, RB)

    arrive(chan(3), ag2, ROWS)
    keep = iota((T, W), 1) < R + 2 * N
    pg = jnp.where(keep, ag2[...].astype(F32), 0.0).astype(BF16)
    act = pre_act[...]
    total = uscan[...] + dot_nt(pg, xwp[...])
    act_grad = total * silu_grad(act)
    apad[:T, :] = act_grad
    apad[T:, :] = jnp.zeros((8, C), F32)

    @pl.when(ms > 0)
    def _():
        halo_copy(apad.at[:8, :], halo_a, 1, before).start()

    xl_f[...] = dot(ut_bf[...], pg[:, :R])
    xl_send[...] = xl_f[...].astype(BF16)
    scatter(seq(2), xl_send, xl_rs, CB)
    sm_f[: 2 * N, :] = dot(pg[:, R:].astype(F32).T.astype(BF16), u_bf[...])[: 2 * N]
    for k in range(4):
        sm_f[3 * N + k : 3 * N + k + 1, :] = jnp.sum(act_grad * xpad[5 + k : 5 + k + T, :], 0, keepdims=True)
    sm_f[3 * N + 4 : 3 * N + 5, :] = jnp.sum(act_grad, 0, keepdims=True)
    g_sum = jnp.zeros((ROWS, LANES), F32)
    for c in range(NC):
        g_sum = g_sum + ag2[c * ROWS : (c + 1) * ROWS, R:].astype(F32)
    gq = g_sum[:4] + g_sum[4:8]
    low_half = iota((1, LANES), 1) < half
    for k in range(2):
        sm_f[3 * N + 7 : 3 * N + 8, k * LANES : (k + 1) * LANES] = jnp.where(
            low_half, pltpu.roll(gq[2 * k : 2 * k + 1], half, 1), gq[2 * k + 1 : 2 * k + 2]
        )
    scatter(seq(3), sm_f, sm_rs, SB)

    @pl.when(ms < NS - 1)
    def _():
        halo_copy(halo_a, halo_a, 1, after).wait_recv()
        apad[T:, :] = halo_a[...]

    total = jnp.zeros((T, C), F32)
    for k in range(4):
        total = total + cw[k : k + 1] * apad[3 - k : 3 - k + T, :]
    xg_o[...] = total.astype(BF16)

    scale = 1.0 / math.sqrt(T * NS)
    at = pl.ds(pl.multiple_of(ms * CB, CB), CB)
    xl_ag[at, :] = collect(seq(2), xl_rs, xl_f[at, :]).astype(BF16)
    spread(seq(4), xl_ag, CB)
    at = pl.ds(pl.multiple_of(ms * SB, SB), SB)
    sm_ag[at, :] = collect(seq(3), sm_rs, sm_f[at, :])
    spread(seq(5), sm_ag, SB)
    arrive(seq(1), dw_ag, RB)
    dwg_o[...] = scale * dw_ag[...].astype(F32)
    arrive(seq(4), xl_ag, CB)
    xpg_o[:, :R] = scale * xl_ag[...].astype(F32)
    arrive(seq(5), sm_ag, SB)
    small = scale * sm_ag[...]
    flipped = small.T
    xpg_o[:, R:] = flipped[:, : 2 * N]
    alg_o[...] = flipped[:, 2 * N : 3 * N]
    cwg_o[...] = small[3 * N : 3 * N + 4]
    cbg_o[...] = small[3 * N + 4 : 3 * N + 5]
    dbg_o[...] = small[3 * N + 5 : 3 * N + 6]
    dsg_o[...] = small[3 * N + 6 : 3 * N + 7]
    dgg_o[...] = small[3 * N + 7 : 3 * N + 8, :R]

    for k, size, src in ((0, ROWS, send1), (1, ROWS, ag1), (2, ROWS, send2), (3, ROWS, ag2)):
        for peer in chan(k).peers():
            chan(k).wait_send(src.at[:size, :], peer)
    for k, size, src in ((0, RB, dw_send), (1, RB, dw_ag), (2, CB, xl_send), (3, SB, sm_f), (4, CB, xl_ag), (5, SB, sm_ag)):
        for peer in seq(k).peers():
            seq(k).wait_send(src.at[:size, :], peer)
    for peer in states(2).peers():
        states(2).wait_send(tot, peer)
    for d in range(1, NS):

        @pl.when(ms + d < NS)
        def _(d=d):
            states(0).wait_send(st_f, ms + d)

        @pl.when(ms - d >= 0)
        def _(d=d):
            states(1).wait_send(st_b, ms - d)

    @pl.when(ms < NS - 1)
    def _():
        halo_copy(halo_x, halo_x, 0, after).wait_send()

    @pl.when(ms > 0)
    def _():
        halo_copy(halo_a, halo_a, 1, before).wait_send()


def per_device(counts, x_in, z_in, grad_out, conv_w, conv_b, xproj_w, dt_w, dt_bias, a_log, d_skip, dt_gain):
    T, C = x_in.shape
    R = dt_w.shape[0]
    N = a_log.shape[1]
    NS, NC = counts
    ROWS = T // NC
    W = R + LANES
    GN = GROUP * N
    SM = 4 * N
    dims = (T, C, NS, NC, R, N)

    def f32(*shape):
        return pltpu.VMEM(shape, F32)

    def b16(*shape):
        return pltpu.VMEM(shape, BF16)

    dma = pltpu.SemaphoreType.DMA
    scratch = dict(
        xpad=f32(T + 8, C), pre_act=f32(T, C), u_bf=b16(T, C), ut_bf=b16(C, T), gy=f32(T, C), gz=f32(T, C),
        xwp=b16(C, W), part=f32(T, W), send1=b16(T, W), rs1=b16(NC, ROWS, W), ag1=b16(T, W),
        low_own=f32(ROWS, R), inv_own=f32(ROWS, LANES),
        pre_soft=f32(T, C), delta=f32(T, C), drive=f32(T, C), bB=f32(T * N, LANES), cB=f32(T * N, LANES),
        a_buf=f32(T * N, C), h_buf=b16((T + 1) * N, C), lam_buf=b16(T * N, C), ha_buf=b16(T * N, C),
        st_f=b16(N, C), st_b=b16(N, C), tot=f32(1, C), in_f=b16(NS, N, C), in_b=b16(NS, N, C),
        in_tot=f32(NS, 1, C), carry_f=f32(N, C), carry_b=f32(N, C),
        e_exp=b16(GN, GROUP), m_b=f32(GN, LANES), m_c=f32(GN, LANES), sel_b=b16(LANES, GN), sel_c=b16(LANES, GN),
        dmask=f32(GROUP, GN), back_b=b16(GN, LANES), back_c=b16(GN, LANES),
        yv=f32(T, C), bcg=f32(T, LANES), uscan=f32(T, C), pregrad=f32(T, C), prehalf=b16(T, C),
        send2=b16(T, W), rs2=b16(NC, ROWS, W), ag2=b16(T, W),
        dw_f=f32(R, C), dw_send=b16(R, C), dw_rs=b16(NS, R // NS, C), dw_ag=b16(R, C),
        xl_f=f32(C, R), xl_send=b16(C, R), xl_rs=b16(NS, C // NS, R), xl_ag=b16(C, R),
        sm_f=f32(SM, C), sm_rs=f32(NS, SM // NS, C), sm_ag=f32(SM, C),
        halo_x=b16(16, C), halo_a=f32(8, C), apad=f32(T + 8, C),
        s_c=dma((4, NC)), r_c=dma((4, NC)), s_st=dma((3, NS)), r_st=dma((3, NS)),
        s_sq=dma((6, NS)), r_sq=dma((6, NS)), s_h=dma((2,)), r_h=dma((2,)),
    )
    S = jax.ShapeDtypeStruct
    out_shape = (
        S((T, C), BF16), S((T, C), BF16), S((4, C), F32), S((1, C), F32), S((C, R + 2 * N), F32),
        S((R, C), F32), S((1, C), F32), S((C, N), F32), S((1, C), F32), S((1, R), F32),
    )
    vmem = pl.BlockSpec(memory_space=pltpu.VMEM)
    out = pl.pallas_call(
        functools.partial(layer_kernel, dims),
        out_shape=out_shape,
        in_specs=[vmem] * 11,
        out_specs=(vmem,) * 10,
        scratch_shapes=list(scratch.values()),
        compiler_params=pltpu.CompilerParams(
            collective_id=0, has_side_effects=True, vmem_limit_bytes=60 * 1024 * 1024
        ),
    )(
        x_in, z_in, grad_out, conv_w, conv_b[None], xproj_w, dt_w, dt_bias[None], a_log, d_skip[None], dt_gain[None],
    )
    xg, zg, cwg, cbg, xpg, dwg, dbg, alg, dsg, dgg = out
    return xg, zg, cwg, cbg[0], xpg, dwg, dbg[0], alg, dsg[0], dgg[0]


def solution(mesh):
    placed = (
        P("seq", "chan"),
        P("seq", "chan"),
        P("seq", "chan"),
        P(None, "chan"),
        P("chan"),
        P("chan", None),
        P(None, "chan"),
        P("chan"),
        P("chan", None),
        P("chan"),
        P(),
    )
    counts = (mesh.shape["seq"], mesh.shape["chan"])
    return jax.shard_map(
        functools.partial(per_device, counts),
        mesh=mesh,
        in_specs=placed,
        out_specs=(
            P("seq", "chan"),
            P("seq", "chan"),
            P(None, "chan"),
            P("chan"),
            P("chan", None),
            P(None, "chan"),
            P("chan"),
            P("chan", None),
            P("chan"),
            P(),
        ),
        check_vma=False,
    )
```

profile of v0, /device:TPU:1, one launch (start us, length us, event | category | flops | bytes accessed | tf_op | source)
XLA Modules:
  0.0 92.6 jit_solution(5257569731261128933)
XLA Ops:
  0.6 0.0 copy-start.1
  0.7 1.6 %copy.22.refs_8_ = f32[512,16]{1,0:T(8,128)} copy(f32[512,16]{0,1:T(8,128)} %param.19) | data formatting | bytes 65536 | tf_op args[8]
  2.3 0.0 copy-done.1
  2.3 0.9 copy.21.refs_5_
  3.2 80.1 %shard_map.186 = (bf16[256,512]{1,0:T(8,128)(2,1)}, bf16[256,512]{1,0:T(8,128)(2,1)}, f32[4,512]{1,0:T(4,128)}, f32[1,512]{1,0:T(1,128)}, f32[512,288]{1,0:T(8,1...) custom-call(bf16[256,512]{1,0:T(8,128)(2,1)} %refs_0_.1, ...), custom_call_target="tpu_custom_call" | custom-call | tf_op jit(solution)/shard_map/pallas_call | solution.py:511
  83.3 1.7 %copy.24 = f32[512,16]{0,1:T(8,128)} copy(f32[512,16]{1,0:T(8,128)} %get-tuple-element.37) | data formatting | bytes 65536
  85.0 0.0 copy-start.3
  85.0 0.0 copy-start.2
  85.0 2.2 %copy.23 = f32[512,288]{0,1:T(8,128)} copy(f32[512,288]{1,0:T(8,128)} %get-tuple-element.34) | data formatting | bytes 1179648
  87.3 0.0 copy-done.3
  87.3 0.0 copy-start
  87.3 0.7 copy.33
  88.0 0.0 copy-done.2
  88.0 0.0 copy-start.4
  88.0 0.7 copy.34
  88.7 0.0 copy-done.4
  88.7 0.0 copy-start.7
  88.7 0.6 copy.35
  89.3 0.1 copy-done.7
  89.4 0.6 copy.36
  89.9 0.0 copy-done
  89.9 0.0 copy-start.6
  89.9 0.8 copy.37
  90.7 0.0 copy-done.6
  90.7 0.0 copy-start.5
  90.7 0.6 copy.38
  91.3 0.1 copy-done.5
  91.4 0.0 copy-start.8
  91.4 0.6 copy.39
  92.0 0.1 copy-done.8
  92.1 0.6 copy.40
Async XLA Ops:
  0.6 1.7 %copy-start.1 = (bf16[512,288]{0,1:T(8,128)(2,1)S(1)}, bf16[512,288]{0,1:T(8,128)(2,1)}, u32[]{:S(2)}) copy-start(bf16[512,288]{0,1:T(8,128)(2,1)} %param.16) | copy-start | bytes 884740
  85.0 2.3 %copy-start.3 = (bf16[256,512]{1,0:T(8,128)(2,1)S(1)}, bf16[256,512]{1,0:T(8,128)(2,1)}, u32[]{:S(2)}) copy-start(bf16[256,512]{1,0:T(8,128)(2,1)} %get-tuple-element.50) | copy-start | bytes 786436
  85.0 3.0 %copy-start.2 = (bf16[256,512]{1,0:T(8,128)(2,1)S(1)}, bf16[256,512]{1,0:T(8,128)(2,1)}, u32[]{:S(2)}) copy-start(bf16[256,512]{1,0:T(8,128)(2,1)} %get-tuple-element.51) | copy-start | bytes 786436
  87.3 2.7 %copy-start = (f32[256,512]{1,0:T(8,128)S(1)}, f32[256,512]{1,0:T(8,128)}, u32[]{:S(2)}) copy-start(f32[256,512]{1,0:T(8,128)} %get-tuple-element.55) | copy-start | bytes 1572868
  88.0 0.7 copy-start.4
  88.7 0.7 copy-start.7
  89.9 0.8 copy-start.6
  90.7 0.7 copy-start.5
  91.4 0.6 copy-start.8
where the time goes:
time: 92.9 us; the launch traced here: 92.6 us
  Pallas kernels  80.1 us (86%)
  local copies, waits for them, and re-layouts  11.8 us (13%)
    pallas_call x1, Pallas kernels, per_device(): pl.pallas_call(functools.partial(layer_kernel, dims), out_shape=out_shape...  80.1 us
    unnamed x30, local copies, waits for them, and re-layouts  11.8 us

commit v1 on v0

--- a/solution.py
+++ b/solution.py
@@ -15,6 +15,7 @@
 F32 = jnp.float32
 BF16 = jnp.bfloat16
 MESH = pl.DeviceIdType.MESH
+VMEM_BYTES = 60 * 1024 * 1024
 
 
 def dot(a, b):
@@ -23,6 +24,10 @@
 
 def dot_nt(a, b):
     return lax.dot_general(a, b, (((1,), (1,)), ((), ())), preferred_element_type=F32)
+
+
+def dot_tn(a, b):
+    return lax.dot_general(a, b, (((0,), (0,)), ((), ())), preferred_element_type=F32)
 
 
 def iota(shape, dim):
@@ -69,20 +74,20 @@
 def layer_kernel(dims, *refs):
     T, C, NS, NC, R, N = dims
     (x_ref, z_ref, g_ref, cw_ref, cb_ref, xw_ref, dw_ref, db_ref, al_ref, ds_ref, dg_ref,
-     xg_o, zg_o, cwg_o, cbg_o, xpg_o, dwg_o, dbg_o, alg_o, dsg_o, dgg_o,
-     xpad, pre_act, u_bf, ut_bf, gy, gz, xwp, part, send1, rs1, ag1, low_own, inv_own,
+     xg_o, zg_o, dw_ag, xl_ag, sm_ag,
+     xpad, pre_act, u_bf, gy, gz, xwp, part, send1, rs1, ag1, low_own, inv_own,
      pre_soft, delta, drive, bB, cB, a_buf, h_buf, lam_buf, ha_buf,
      st_f, st_b, tot, in_f, in_b, in_tot, carry_f, carry_b,
      e_exp, m_b, m_c, sel_b, sel_c, dmask, back_b, back_c,
      yv, bcg, uscan, pregrad, prehalf, send2, rs2, ag2,
-     dw_f, dw_send, dw_rs, dw_ag, xl_f, xl_send, xl_rs, xl_ag, sm_f, sm_rs, sm_ag,
+     dw_f, dw_send, dw_rs, xl_f, xl_send, xl_rs, sm_f, sm_rs,
      halo_x, halo_a, apad,
      s_c, r_c, s_st, r_st, s_sq, r_sq, s_h, r_h) = refs
     ROWS = T // NC
     W = R + LANES
     NB = T // GROUP
     GN = GROUP * N
-    RB, CB = R // NS, C // NS
+    RB = R // NS
     SM = sm_f.shape[0]
     SB = SM // NS
     ms, mc = lax.axis_index("seq"), lax.axis_index("chan")
@@ -112,8 +117,8 @@
     sel_b[...] = ((k_row == col_n) | (k_row == col_n + 2 * N)).astype(F32).astype(BF16)
     sel_c[...] = ((k_row == col_n + N) | (k_row == col_n + 3 * N)).astype(F32).astype(BF16)
     dmask[...] = (iota((GROUP, GN), 1) // N == iota((GROUP, GN), 0)).astype(F32)
-    xwp[...] = jnp.zeros_like(xwp)
-    xwp[:, : R + 2 * N] = xw_ref[...]
+    xwp[: R + 2 * N, :] = xw_ref[...]
+    xwp[R + 2 * N :, :] = jnp.zeros((LANES - 2 * N, C), BF16)
 
     xpad[:8, :] = jnp.zeros((8, C), F32)
     xpad[8:, :] = x_ref[...].astype(F32)
@@ -156,7 +161,7 @@
     act = pre_act[...]
     u_bf[...] = (act * jax.nn.sigmoid(act)).astype(BF16)
 
-    part[...] = dot(u_bf[...], xwp[...])
+    part[...] = dot_nt(u_bf[...], xwp[...])
     send1[...] = part[...].astype(BF16)
 
     def my_rows(ref):
@@ -185,8 +190,7 @@
             ex.wait_recv(block(buf, peer, size), peer)
 
     scatter(chan(0), send1, rs1, ROWS)
-    ut_bf[...] = u_bf[...].astype(F32).T.astype(BF16)
-    rate = -jnp.exp(al_ref[...].T)
+    rate = -jnp.exp(al_ref[...])
     rate2 = rate * LOG2E
     proj = collect(chan(0), rs1, my_rows(part))
     low = proj[:, :R]
@@ -342,7 +346,7 @@
     send2[...] = part[...].astype(BF16)
     scatter(chan(2), send2, rs2, ROWS)
 
-    dw_f[...] = dot(ag1[:, :R].astype(F32).T.astype(BF16), prehalf[...])
+    dw_f[...] = dot_tn(ag1[:, :R], prehalf[...])
     dw_send[...] = dw_f[...].astype(BF16)
     scatter(seq(0), dw_send, dw_rs, RB)
     u32 = u_bf[...].astype(F32)
@@ -379,7 +383,7 @@
     keep = iota((T, W), 1) < R + 2 * N
     pg = jnp.where(keep, ag2[...].astype(F32), 0.0).astype(BF16)
     act = pre_act[...]
-    total = uscan[...] + dot_nt(pg, xwp[...])
+    total = uscan[...] + dot(pg, xwp[...])
     act_grad = total * silu_grad(act)
     apad[:T, :] = act_grad
     apad[T:, :] = jnp.zeros((8, C), F32)
@@ -388,10 +392,10 @@
     def _():
         halo_copy(apad.at[:8, :], halo_a, 1, before).start()
 
-    xl_f[...] = dot(ut_bf[...], pg[:, :R])
-    xl_send[...] = xl_f[...].astype(BF16)
-    scatter(seq(2), xl_send, xl_rs, CB)
-    sm_f[: 2 * N, :] = dot(pg[:, R:].astype(F32).T.astype(BF16), u_bf[...])[: 2 * N]
+    xl_f[...] = dot_tn(pg, u_bf[...])
+    xl_send[...] = xl_f[:R, :].astype(BF16)
+    scatter(seq(2), xl_send, xl_rs, RB)
+    sm_f[: 2 * N, :] = xl_f[R : R + 2 * N, :]
     for k in range(4):
         sm_f[3 * N + k : 3 * N + k + 1, :] = jnp.sum(act_grad * xpad[5 + k : 5 + k + T, :], 0, keepdims=True)
     sm_f[3 * N + 4 : 3 * N + 5, :] = jnp.sum(act_grad, 0, keepdims=True)
@@ -416,32 +420,20 @@
         total = total + cw[k : k + 1] * apad[3 - k : 3 - k + T, :]
     xg_o[...] = total.astype(BF16)
 
-    scale = 1.0 / math.sqrt(T * NS)
-    at = pl.ds(pl.multiple_of(ms * CB, CB), CB)
+    at = pl.ds(pl.multiple_of(ms * RB, RB), RB)
     xl_ag[at, :] = collect(seq(2), xl_rs, xl_f[at, :]).astype(BF16)
-    spread(seq(4), xl_ag, CB)
+    spread(seq(4), xl_ag, RB)
     at = pl.ds(pl.multiple_of(ms * SB, SB), SB)
     sm_ag[at, :] = collect(seq(3), sm_rs, sm_f[at, :])
     spread(seq(5), sm_ag, SB)
     arrive(seq(1), dw_ag, RB)
-    dwg_o[...] = scale * dw_ag[...].astype(F32)
-    arrive(seq(4), xl_ag, CB)
-    xpg_o[:, :R] = scale * xl_ag[...].astype(F32)
+    arrive(seq(4), xl_ag, RB)
     arrive(seq(5), sm_ag, SB)
-    small = scale * sm_ag[...]
-    flipped = small.T
-    xpg_o[:, R:] = flipped[:, : 2 * N]
-    alg_o[...] = flipped[:, 2 * N : 3 * N]
-    cwg_o[...] = small[3 * N : 3 * N + 4]
-    cbg_o[...] = small[3 * N + 4 : 3 * N + 5]
-    dbg_o[...] = small[3 * N + 5 : 3 * N + 6]
-    dsg_o[...] = small[3 * N + 6 : 3 * N + 7]
-    dgg_o[...] = small[3 * N + 7 : 3 * N + 8, :R]
 
     for k, size, src in ((0, ROWS, send1), (1, ROWS, ag1), (2, ROWS, send2), (3, ROWS, ag2)):
         for peer in chan(k).peers():
             chan(k).wait_send(src.at[:size, :], peer)
-    for k, size, src in ((0, RB, dw_send), (1, RB, dw_ag), (2, CB, xl_send), (3, SB, sm_f), (4, CB, xl_ag), (5, SB, sm_ag)):
+    for k, size, src in ((0, RB, dw_send), (1, RB, dw_ag), (2, RB, xl_send), (3, SB, sm_f), (4, RB, xl_ag), (5, SB, sm_ag)):
         for peer in seq(k).peers():
             seq(k).wait_send(src.at[:size, :], peer)
     for peer in states(2).peers():
@@ -463,6 +455,22 @@
     @pl.when(ms > 0)
     def _():
         halo_copy(halo_a, halo_a, 1, before).wait_send()
+
+
+def finish_kernel(dims, xg, zg, dw_sum, xl_sum, sm_sum, xg_o, zg_o, cwg_o, cbg_o, xpg_o, dwg_o, dbg_o, alg_o, dsg_o, dgg_o):
+    T, C, NS, NC, R, N = dims
+    scale = 1.0 / math.sqrt(T * NS)
+    xg_o[...] = xg[...]
+    zg_o[...] = zg[...]
+    dwg_o[...] = scale * dw_sum[...].astype(F32)
+    xpg_o[:R, :] = scale * xl_sum[...].astype(F32)
+    xpg_o[R:, :] = scale * sm_sum[: 2 * N, :]
+    alg_o[...] = scale * sm_sum[2 * N : 3 * N, :]
+    cwg_o[...] = scale * sm_sum[3 * N : 3 * N + 4, :]
+    cbg_o[...] = scale * sm_sum[3 * N + 4 : 3 * N + 5, :]
+    dbg_o[...] = scale * sm_sum[3 * N + 5 : 3 * N + 6, :]
+    dsg_o[...] = scale * sm_sum[3 * N + 6 : 3 * N + 7, :]
+    dgg_o[...] = scale * sm_sum[3 * N + 7 : 3 * N + 8, :R]
 
 
 def per_device(counts, x_in, z_in, grad_out, conv_w, conv_b, xproj_w, dt_w, dt_bias, a_log, d_skip, dt_gain):
@@ -484,8 +492,8 @@
 
     dma = pltpu.SemaphoreType.DMA
     scratch = dict(
-        xpad=f32(T + 8, C), pre_act=f32(T, C), u_bf=b16(T, C), ut_bf=b16(C, T), gy=f32(T, C), gz=f32(T, C),
-        xwp=b16(C, W), part=f32(T, W), send1=b16(T, W), rs1=b16(NC, ROWS, W), ag1=b16(T, W),
+        xpad=f32(T + 8, C), pre_act=f32(T, C), u_bf=b16(T, C), gy=f32(T, C), gz=f32(T, C),
+        xwp=b16(W, C), part=f32(T, W), send1=b16(T, W), rs1=b16(NC, ROWS, W), ag1=b16(T, W),
         low_own=f32(ROWS, R), inv_own=f32(ROWS, LANES),
         pre_soft=f32(T, C), delta=f32(T, C), drive=f32(T, C), bB=f32(T * N, LANES), cB=f32(T * N, LANES),
         a_buf=f32(T * N, C), h_buf=b16((T + 1) * N, C), lam_buf=b16(T * N, C), ha_buf=b16(T * N, C),
@@ -495,33 +503,38 @@
         dmask=f32(GROUP, GN), back_b=b16(GN, LANES), back_c=b16(GN, LANES),
         yv=f32(T, C), bcg=f32(T, LANES), uscan=f32(T, C), pregrad=f32(T, C), prehalf=b16(T, C),
         send2=b16(T, W), rs2=b16(NC, ROWS, W), ag2=b16(T, W),
-        dw_f=f32(R, C), dw_send=b16(R, C), dw_rs=b16(NS, R // NS, C), dw_ag=b16(R, C),
-        xl_f=f32(C, R), xl_send=b16(C, R), xl_rs=b16(NS, C // NS, R), xl_ag=b16(C, R),
-        sm_f=f32(SM, C), sm_rs=f32(NS, SM // NS, C), sm_ag=f32(SM, C),
+        dw_f=f32(R, C), dw_send=b16(R, C), dw_rs=b16(NS, R // NS, C),
+        xl_f=f32(W, C), xl_send=b16(R, C), xl_rs=b16(NS, R // NS, C),
+        sm_f=f32(SM, C), sm_rs=f32(NS, SM // NS, C),
         halo_x=b16(16, C), halo_a=f32(8, C), apad=f32(T + 8, C),
         s_c=dma((4, NC)), r_c=dma((4, NC)), s_st=dma((3, NS)), r_st=dma((3, NS)),
         s_sq=dma((6, NS)), r_sq=dma((6, NS)), s_h=dma((2,)), r_h=dma((2,)),
     )
     S = jax.ShapeDtypeStruct
-    out_shape = (
-        S((T, C), BF16), S((T, C), BF16), S((4, C), F32), S((1, C), F32), S((C, R + 2 * N), F32),
-        S((R, C), F32), S((1, C), F32), S((C, N), F32), S((1, C), F32), S((1, R), F32),
-    )
     vmem = pl.BlockSpec(memory_space=pltpu.VMEM)
-    out = pl.pallas_call(
+    raw = pl.pallas_call(
         functools.partial(layer_kernel, dims),
-        out_shape=out_shape,
+        out_shape=(S((T, C), BF16), S((T, C), BF16), S((R, C), BF16), S((R, C), BF16), S((SM, C), F32)),
         in_specs=[vmem] * 11,
-        out_specs=(vmem,) * 10,
+        out_specs=(vmem,) * 5,
         scratch_shapes=list(scratch.values()),
         compiler_params=pltpu.CompilerParams(
-            collective_id=0, has_side_effects=True, vmem_limit_bytes=60 * 1024 * 1024
+            collective_id=0, has_side_effects=True, vmem_limit_bytes=VMEM_BYTES
         ),
     )(
-        x_in, z_in, grad_out, conv_w, conv_b[None], xproj_w, dt_w, dt_bias[None], a_log, d_skip[None], dt_gain[None],
+        x_in, z_in, grad_out, conv_w, conv_b[None], xproj_w.T, dt_w, dt_bias[None], a_log.T, d_skip[None], dt_gain[None],
     )
-    xg, zg, cwg, cbg, xpg, dwg, dbg, alg, dsg, dgg = out
-    return xg, zg, cwg, cbg[0], xpg, dwg, dbg[0], alg, dsg[0], dgg[0]
+    xg, zg, cwg, cbg, xpg, dwg, dbg, alg, dsg, dgg = pl.pallas_call(
+        functools.partial(finish_kernel, dims),
+        out_shape=(
+            S((T, C), BF16), S((T, C), BF16), S((4, C), F32), S((1, C), F32), S((R + 2 * N, C), F32),
+            S((R, C), F32), S((1, C), F32), S((N, C), F32), S((1, C), F32), S((1, R), F32),
+        ),
+        in_specs=[vmem] * 5,
+        out_specs=(vmem,) * 10,
+        compiler_params=pltpu.CompilerParams(vmem_limit_bytes=VMEM_BYTES),
+    )(*raw)
+    return xg, zg, cwg, cbg[0], xpg.T, dwg, dbg[0], alg.T, dsg[0], dgg[0]
 
 
 def solution(mesh):

time: 92.9 us -> 83 us (0.89)
  local copies, waits for them, and re-layouts: 11.8 us -> 0 us
  Pallas kernels: 80.1 us -> 82.2 us
    unnamed x30 -> x0, local copies, waits for them, and re-layouts: 11.8 us -> none
    pallas_call x1 -> x2, Pallas kernels: 80.1 us -> 82.2 us  [the longest x1 79.8 us: per_device(): pl.pallas_call(functools.partial(layer_kernel, dims), out_shape=(S((T, C)...]
where the time goes in v1:
time: 83 us; the launch traced here: 82.9 us
  Pallas kernels  82.2 us (99%)
    pallas_call x1, Pallas kernels, per_device(): pl.pallas_call(functools.partial(layer_kernel, dims), out_shape=(S((T, C)...  79.8 us
    pallas_call x1, Pallas kernels, per_device(): pl.pallas_call(functools.partial(finish_kernel, dims), out_shape=(S((T, C...  2.42 us

profile of v1, /device:TPU:1, one launch (start us, length us, event | category | flops | bytes accessed | tf_op | source)
XLA Modules:
  0.0 82.9 jit_solution(130654980866073104)
XLA Ops:
  0.6 79.8 %shard_map.186 = (bf16[256,512]{1,0:T(8,128)(2,1)}, bf16[256,512]{1,0:T(8,128)(2,1)}, bf16[256,512]{1,0:T(8,128)(2,1)}, bf16[256,512]{1,0:T(8,128)(2,1)}, f32[64,512]{1,0:T(8,128)}) custom-call(bf16[256,512]{1,0:T(8,128)(2,1)} %refs_0_.1, bf16[256,512]{1,0:T(8,128)(2,1)} %refs_1_.1, bf16[256,512]{1,0:T(8,128)(2,1)} %refs_2_.1, f32[4,512]{1,0:T(4,128)} %refs_3_.1, ...), custom_call_target="tpu_custom_call" | custom-call | tf_op jit(solution)/shard_map/pallas_call | solution.py:515
  80.4 2.4 %shard_map.187 = (bf16[256,512]{1,0:T(8,128)(2,1)}, bf16[256,512]{1,0:T(8,128)(2,1)}, f32[4,512]{1,0:T(4,128)}, f32[1,512]{1,0:T(1,128)}, f32[288,512]{1,0:T(8,1...) custom-call(bf16[256,512]{1,0:T(8,128)(2,1)} %get-tuple-element.25.x, ...), custom_call_target="tpu_custom_call" | custom-call | tf_op jit(solution)/shard_map/pallas_call | solution.py:527

commit v2 on v1

--- a/solution.py
+++ b/solution.py
@@ -16,6 +16,8 @@
 BF16 = jnp.bfloat16
 MESH = pl.DeviceIdType.MESH
 VMEM_BYTES = 60 * 1024 * 1024
+CHUNK = 4
+UNROLL_FP = UNROLL_BP = UNROLL_F = UNROLL_B = 16
 
 
 def dot(a, b):
@@ -73,18 +75,20 @@
 
 def layer_kernel(dims, *refs):
     T, C, NS, NC, R, N = dims
-    (x_ref, z_ref, g_ref, cw_ref, cb_ref, xw_ref, dw_ref, db_ref, al_ref, ds_ref, dg_ref,
-     xg_o, zg_o, dw_ag, xl_ag, sm_ag,
-     xpad, pre_act, u_bf, gy, gz, xwp, part, send1, rs1, ag1, low_own, inv_own,
+    hbm, refs = refs[:11], refs[11:]
+    (xg_o, zg_o, dw_ag, xl_ag, sm_ag,
+     x_ref, z_ref, g_ref, cw_ref, cb_ref, xw_ref, dw_ref, db_ref, al_ref, ds_ref, dg_ref,
+     xpad, pre_act, act_slope, u_bf, gy, gz, part, send1, rs1, ag1, low_own, inv_own,
      pre_soft, delta, drive, bB, cB, a_buf, h_buf, lam_buf, ha_buf,
      st_f, st_b, tot, in_f, in_b, in_tot, carry_f, carry_b,
      e_exp, m_b, m_c, sel_b, sel_c, dmask, back_b, back_c,
-     yv, bcg, uscan, pregrad, prehalf, send2, rs2, ag2,
+     bcg, uscan, pregrad, prehalf, send2, rs2, ag2,
      dw_f, dw_send, dw_rs, xl_f, xl_send, xl_rs, sm_f, sm_rs,
      halo_x, halo_a, apad,
-     s_c, r_c, s_st, r_st, s_sq, r_sq, s_h, r_h) = refs
+     s_in, s_c, r_c, s_st, r_st, s_sq, r_sq, s_h, r_h) = refs
     ROWS = T // NC
     W = R + LANES
+    P2 = R + 2 * N
     NB = T // GROUP
     GN = GROUP * N
     RB = R // NS
@@ -106,7 +110,96 @@
         pl.semaphore_signal(barrier, inc=1, device_id={"chan": lax.rem(mc + d, NC)}, device_id_type=MESH)
     for d in range(1, NS):
         pl.semaphore_signal(barrier, inc=1, device_id={"seq": lax.rem(ms + d, NS)}, device_id_type=MESH)
-
+    local = (x_ref, z_ref, g_ref, cw_ref, cb_ref, xw_ref, dw_ref, db_ref, al_ref, ds_ref, dg_ref)
+    fetch = [pltpu.make_async_copy(hbm[k], local[k], s_in.at[k]) for k in range(11)]
+    for k in (0, 3, 4, 5, 1, 2, 6, 7, 8, 9, 10):
+        fetch[k].start()
+
+    xpad[:8, :] = jnp.zeros((8, C), F32)
+    for k in (0, 3, 4):
+        fetch[k].wait()
+    xpad[8:, :] = x_ref[...].astype(F32)
+    cw = cw_ref[...]
+
+    def conv(first, count):
+        total = jnp.broadcast_to(cb_ref[...], (count, C))
+        for k in range(4):
+            total = total + cw[k : k + 1] * xpad[first + 5 + k : first + 5 + k + count, :]
+        pre_act[first : first + count, :] = total
+        u_bf[first : first + count, :] = (total * jax.nn.sigmoid(total)).astype(BF16)
+
+    def project(first, count):
+        sums = dot_nt(u_bf[first : first + count, :], xw_ref[...])
+        part[first : first + count, :R] = sums[:, :R]
+        part[first : first + count, R:P2] = sums[:, R:P2]
+        send1[first : first + count, :R] = sums[:, :R].astype(BF16)
+        send1[first : first + count, R:P2] = sums[:, R:P2].astype(BF16)
+
+    def halo_copy(src, dst, k, peer):
+        return pltpu.make_async_remote_copy(
+            src_ref=src, dst_ref=dst, send_sem=s_h.at[k], recv_sem=r_h.at[k],
+            device_id={"seq": peer}, device_id_type=MESH,
+        )
+
+    def block(ref, i, size):
+        return ref.at[pl.ds(pl.multiple_of(i * size, size), size), :]
+
+    def scatter(ex, src, slots, size):
+        for peer in ex.peers():
+            ex.send(block(src, peer, size), slots.at[ex.me], peer)
+
+    def collect(ex, slots, own):
+        for peer in ex.peers():
+            ex.wait_recv(slots.at[peer], peer)
+        for peer in ex.peers():
+            own = own + slots[peer].astype(F32)
+        return own
+
+    def spread(ex, buf, size):
+        for peer in ex.peers():
+            ex.send(block(buf, ex.me, size), block(buf, ex.me, size), peer)
+
+    def arrive(ex, buf, size):
+        for peer in ex.peers():
+            ex.wait_recv(block(buf, peer, size), peer)
+
+    after, before = lax.rem(ms + 1, NS), lax.rem(ms + NS - 1, NS)
+    pl.semaphore_wait(barrier, NC + NS - 2)
+
+    @pl.when(ms < NS - 1)
+    def _():
+        halo_copy(x_ref.at[T - 16 :, :], halo_x, 0, after).start()
+
+    part[:, R:] = jnp.zeros((T, LANES), F32)
+    send1[:, R:] = jnp.zeros((T, LANES), BF16)
+    conv(0, T)
+    fetch[5].wait()
+    project(ROWS, T - ROWS)
+    for peer in chan(0).peers():
+
+        @pl.when(peer != 0)
+        def _(peer=peer):
+            chan(0).send(block(send1, peer, ROWS), rs1.at[mc], peer)
+
+    @pl.when(ms > 0)
+    def _():
+        halo_copy(halo_x, halo_x, 0, before).wait_recv()
+        xpad[:8, :] = halo_x[...].astype(F32)[8:16]
+        conv(0, 16)
+
+    project(0, ROWS)
+
+    @pl.when(mc != 0)
+    def _():
+        chan(0).send(block(send1, 0, ROWS), rs1.at[mc], 0)
+
+    for k in (1, 2, 6, 7, 8, 9, 10):
+        fetch[k].wait()
+    gate = z_ref[...].astype(F32)
+    cot = g_ref[...].astype(F32)
+    sig = jax.nn.sigmoid(gate)
+    gy[...] = cot * gate * sig
+    gz[...] = cot * sig * (1.0 + gate * (1.0 - sig))
     e_exp[...] = (iota((GN, GROUP), 0) // N == iota((GN, GROUP), 1)).astype(F32).astype(BF16)
     row_n, lane = iota((GN, LANES), 0) % N, iota((GN, LANES), 1)
     m_b[...] = ((lane == row_n) | (lane == row_n + 2 * N)).astype(F32)
@@ -117,81 +210,12 @@
     sel_b[...] = ((k_row == col_n) | (k_row == col_n + 2 * N)).astype(F32).astype(BF16)
     sel_c[...] = ((k_row == col_n + N) | (k_row == col_n + 3 * N)).astype(F32).astype(BF16)
     dmask[...] = (iota((GROUP, GN), 1) // N == iota((GROUP, GN), 0)).astype(F32)
-    xwp[: R + 2 * N, :] = xw_ref[...]
-    xwp[R + 2 * N :, :] = jnp.zeros((LANES - 2 * N, C), BF16)
-
-    xpad[:8, :] = jnp.zeros((8, C), F32)
-    xpad[8:, :] = x_ref[...].astype(F32)
-    cw = cw_ref[...]
-
-    def conv(first, count):
-        total = jnp.broadcast_to(cb_ref[...], (count, C))
-        for k in range(4):
-            total = total + cw[k : k + 1] * xpad[first + 5 + k : first + 5 + k + count, :]
-        return total
-
-    pre_act[...] = conv(0, T)
-    pl.semaphore_wait(barrier, NC + NS - 2)
-    halo = Exchange("seq", NS, ms, s_h, r_h)
-
-    def halo_copy(src, dst, k, peer):
-        return pltpu.make_async_remote_copy(
-            src_ref=src, dst_ref=dst, send_sem=s_h.at[k], recv_sem=r_h.at[k],
-            device_id={"seq": peer}, device_id_type=MESH,
-        )
-
-    after, before = lax.rem(ms + 1, NS), lax.rem(ms + NS - 1, NS)
-
-    @pl.when(ms < NS - 1)
-    def _():
-        halo_copy(x_ref.at[T - 16 :, :], halo_x, 0, after).start()
-
-    gate = z_ref[...].astype(F32)
-    cot = g_ref[...].astype(F32)
-    sig = jax.nn.sigmoid(gate)
-    gy[...] = cot * gate * sig
-    gz[...] = cot * sig * (1.0 + gate * (1.0 - sig))
-
-    @pl.when(ms > 0)
-    def _():
-        halo_copy(halo_x, halo_x, 0, before).wait_recv()
-        xpad[:8, :] = halo_x[...].astype(F32)[8:16]
-        pre_act[:8, :] = conv(0, 8)
-
-    act = pre_act[...]
-    u_bf[...] = (act * jax.nn.sigmoid(act)).astype(BF16)
-
-    part[...] = dot_nt(u_bf[...], xwp[...])
-    send1[...] = part[...].astype(BF16)
+    rate = -jnp.exp(al_ref[...])
+    rate2 = rate * LOG2E
 
     def my_rows(ref):
         return ref[pl.ds(pl.multiple_of(mc * ROWS, ROWS), ROWS), :]
 
-    def block(ref, i, size):
-        return ref.at[pl.ds(pl.multiple_of(i * size, size), size), :]
-
-    def scatter(ex, src, slots, size):
-        for peer in ex.peers():
-            ex.send(block(src, peer, size), slots.at[ex.me], peer)
-
-    def collect(ex, slots, own):
-        for peer in ex.peers():
-            ex.wait_recv(slots.at[peer], peer)
-        for peer in ex.peers():
-            own = own + slots[peer].astype(F32)
-        return own
-
-    def spread(ex, buf, size):
-        for peer in ex.peers():
-            ex.send(block(buf, ex.me, size), block(buf, ex.me, size), peer)
-
-    def arrive(ex, buf, size):
-        for peer in ex.peers():
-            ex.wait_recv(block(buf, peer, size), peer)
-
-    scatter(chan(0), send1, rs1, ROWS)
-    rate = -jnp.exp(al_ref[...])
-    rate2 = rate * LOG2E
     proj = collect(chan(0), rs1, my_rows(part))
     low = proj[:, :R]
     inv = lax.rsqrt(jnp.mean(low * low, -1, keepdims=True) + EPS)
@@ -204,6 +228,7 @@
     ag1[mine, :R] = (low * inv * dg_ref[...]).astype(BF16)
     ag1[mine, R:] = tail.astype(BF16)
     spread(chan(1), ag1, ROWS)
+    act_slope[...] = silu_grad(pre_act[...])
     arrive(chan(1), ag1, ROWS)
 
     soft = dot(ag1[:, :R], dw_ref[...]) + db_ref[...]
@@ -215,17 +240,20 @@
     for peer in states(2).peers():
         states(2).send(tot, in_tot.at[ms], peer)
 
+    def tokens(i, count=GROUP):
+        return pl.ds(pl.multiple_of(i * count, count), count)
+
     ones = jnp.ones((LANES, LANES), BF16)
 
     def widen(i, carry):
-        rows = ag1[pl.ds(pl.multiple_of(i * GROUP, GROUP), GROUP), R:]
-        spread_rows = dot(e_exp[...], rows)
-        at = pl.ds(pl.multiple_of(i * GN, GN), GN)
-        bB[at, :] = dot((spread_rows * m_b[...]).astype(BF16), ones)
-        cB[at, :] = dot((spread_rows * m_c[...]).astype(BF16), ones)
+        spread_rows = [dot(e_exp[...], ag1[tokens(i * CHUNK + k), R:]) for k in range(CHUNK)]
+        for k in range(CHUNK):
+            at = pl.ds(pl.multiple_of((i * CHUNK + k) * GN, GN), GN)
+            bB[at, :] = dot((spread_rows[k] * m_b[...]).astype(BF16), ones)
+            cB[at, :] = dot((spread_rows[k] * m_c[...]).astype(BF16), ones)
         return carry
 
-    lax.fori_loop(0, NB, widen, 0)
+    lax.fori_loop(0, NB // CHUNK, widen, 0)
 
     def row(ref, t):
         return ref[pl.ds(t, 1), :]
@@ -239,14 +267,14 @@
     zero_state = jnp.zeros((N, C), F32)
 
     def forward_part(i, h):
-        for j in range(GROUP):
-            t = i * GROUP + j
+        for j in range(UNROLL_FP):
+            t = i * UNROLL_FP + j
             a = jnp.exp2(row(delta, t) * rate2)
             a_buf[state_at(t), :] = a
             h = a * h + row(drive, t) * wide(bB, t)
         return h
 
-    st_f[...] = lax.fori_loop(0, NB, forward_part, zero_state).astype(BF16)
+    st_f[...] = lax.fori_loop(0, T // UNROLL_FP, forward_part, zero_state).astype(BF16)
     for d in range(1, NS):
 
         @pl.when(ms + d < NS)
@@ -254,12 +282,12 @@
             states(0).send(st_f, in_f.at[ms], ms + d)
 
     def backward_part(i, g):
-        for j in range(GROUP):
-            t = T - 1 - (i * GROUP + j)
+        for j in range(UNROLL_BP):
+            t = T - 1 - (i * UNROLL_BP + j)
             g = a_buf[state_at(t), :] * (row(gy, t) * wide(cB, t) + g)
         return g
 
-    st_b[...] = lax.fori_loop(0, NB, backward_part, zero_state).astype(BF16)
+    st_b[...] = lax.fori_loop(0, T // UNROLL_BP, backward_part, zero_state).astype(BF16)
     for d in range(1, NS):
 
         @pl.when(ms - d >= 0)
@@ -280,27 +308,25 @@
     h_buf[:N, :] = start.astype(BF16)
 
     def forward(i, h):
-        for j in range(GROUP):
-            t = i * GROUP + j
+        for j in range(UNROLL_F):
+            t = i * UNROLL_F + j
             h = a_buf[state_at(t), :] * h + row(drive, t) * wide(bB, t)
             h_buf[state_at(t + 1), :] = h.astype(BF16)
         return h
 
-    lax.fori_loop(0, NB, forward, start)
-
-    def tokens(i):
-        return pl.ds(pl.multiple_of(i * GROUP, GROUP), GROUP)
+    lax.fori_loop(0, T // UNROLL_F, forward, start)
+
+    def state_rows(k):
+        return h_buf[pl.ds(pl.multiple_of(k * GN + N, N), GN), :]
 
     def after_forward(i, carry):
-        coef = ag1[tokens(i), R:]
-        h_rows = h_buf[pl.ds(pl.multiple_of(i * GN + N, N), GN), :]
-        c_diag = (dot(coef, sel_c[...]) * dmask[...]).astype(BF16)
-        yv[tokens(i), :] = dot(c_diag, h_rows)
-        c_all = dot_nt(gy[tokens(i), :].astype(BF16), h_rows) * dmask[...]
-        bcg[tokens(i), :] = dot(c_all.astype(BF16), back_c[...])
+        for k in range(CHUNK):
+            k = i * CHUNK + k
+            c_all = dot_nt(gy[tokens(k), :].astype(BF16), state_rows(k)) * dmask[...]
+            bcg[tokens(k), :] = dot(c_all.astype(BF16), back_c[...])
         return carry
 
-    lax.fori_loop(0, NB, after_forward, 0)
+    lax.fori_loop(0, NB // CHUNK, after_forward, 0)
 
     carry_b[...] = zero_state
     for s in range(NS - 1, 0, -1):
@@ -310,51 +336,83 @@
             states(1).wait_recv(in_b.at[s], s)
             carry_b[...] = jnp.exp2(in_tot[s] * rate2) * carry_b[...] + in_b[s].astype(F32)
 
-    def backward(i, carry):
-        g, acc = carry
-        for j in range(GROUP):
-            t = T - 1 - (i * GROUP + j)
-            lam = row(gy, t) * wide(cB, t) + g
-            g = a_buf[state_at(t), :] * lam
-            hold = g * h_buf[state_at(t), :].astype(F32)
-            acc = acc + hold * row(delta, t)
-            lam_buf[state_at(t), :] = lam.astype(BF16)
-            ha_buf[state_at(t), :] = (hold * rate).astype(BF16)
-        return g, acc
-
-    _, rate_sum = lax.fori_loop(0, NB, backward, (carry_b[...], zero_state))
-
-    def after_backward(i, carry):
-        coef = ag1[tokens(i), R:]
-        at = pl.ds(pl.multiple_of(i * GN, GN), GN)
-        lam_rows = lam_buf[at, :]
-        b_diag = (dot(coef, sel_b[...]) * dmask[...]).astype(BF16)
-        adj_b = dot(b_diag, lam_rows)
-        by_rate = dot(dmask[...].astype(BF16), ha_buf[at, :])
-        b_all = dot_nt(drive[tokens(i), :].astype(BF16), lam_rows) * dmask[...]
-        bcg[tokens(i), :] = bcg[tokens(i), :] + dot(b_all.astype(BF16), back_b[...])
-        pre = (by_rate + adj_b * u_bf[tokens(i), :].astype(F32)) * jax.nn.sigmoid(pre_soft[tokens(i), :])
-        pregrad[tokens(i), :] = pre
-        prehalf[tokens(i), :] = pre.astype(BF16)
-        uscan[tokens(i), :] = ds_ref[...] * gy[tokens(i), :] + delta[tokens(i), :] * adj_b
-        return carry
-
-    lax.fori_loop(0, NB, after_backward, 0)
-
-    part[:, :R] = dot_nt(prehalf[...], dw_ref[...])
-    part[:, R:] = bcg[...]
-    send2[...] = part[...].astype(BF16)
-    scatter(chan(2), send2, rs2, ROWS)
+    CT = CHUNK * GROUP
+
+    def backward_chunk(i, g):
+        c = NB // CHUNK - 1 - i
+
+        def backward(m, g):
+            for j in range(UNROLL_B):
+                t = c * CT + CT - 1 - (m * UNROLL_B + j)
+                lam = row(gy, t) * wide(cB, t) + g
+                g = a_buf[state_at(t), :] * lam
+                hold = g * h_buf[state_at(t), :].astype(F32)
+                lam_buf[state_at(t), :] = lam.astype(BF16)
+                ha_buf[state_at(t), :] = (hold * rate).astype(BF16)
+            return g
+
+        g = lax.fori_loop(0, CT // UNROLL_B, backward, g)
+        at = tokens(c, CT)
+        adj_b, by_rate, b_grad = [], [], []
+        for k in range(CHUNK):
+            k = c * CHUNK + k
+            states_k = pl.ds(pl.multiple_of(k * GN, GN), GN)
+            lam_rows = lam_buf[states_k, :]
+            b_diag = (dot(ag1[tokens(k), R:], sel_b[...]) * dmask[...]).astype(BF16)
+            adj_b.append(dot(b_diag, lam_rows))
+            by_rate.append(dot(dmask[...].astype(BF16), ha_buf[states_k, :]))
+            b_all = dot_nt(drive[tokens(k), :].astype(BF16), lam_rows) * dmask[...]
+            b_grad.append(dot(b_all.astype(BF16), back_b[...]))
+        adj_b = jnp.concatenate(adj_b, 0)
+        pre = (jnp.concatenate(by_rate, 0) + adj_b * u_bf[at, :].astype(F32)) * jax.nn.sigmoid(pre_soft[at, :])
+        pregrad[at, :] = pre
+        half = pre.astype(BF16)
+        prehalf[at, :] = half
+        uscan[at, :] = ds_ref[...] * gy[at, :] + delta[at, :] * adj_b
+        normed = dot_nt(half, dw_ref[...])
+        tail = bcg[at, :] + jnp.concatenate(b_grad, 0)
+        part[at, :R] = normed
+        part[at, R:] = tail
+        send2[at, :R] = normed.astype(BF16)
+        send2[at, R:] = tail.astype(BF16)
+        for k in range(CHUNK):
+            owner = c * CHUNK + k
+
+            @pl.when(owner != mc)
+            def _(owner=owner):
+                chan(2).send(block(send2, owner, ROWS), rs2.at[mc], owner)
+
+        return g
+
+    lax.fori_loop(0, NB // CHUNK, backward_chunk, carry_b[...])
 
     dw_f[...] = dot_tn(ag1[:, :R], prehalf[...])
     dw_send[...] = dw_f[...].astype(BF16)
     scatter(seq(0), dw_send, dw_rs, RB)
-    u32 = u_bf[...].astype(F32)
-    zg_o[...] = (gz[...] * (yv[...] + ds_ref[...] * u32)).astype(BF16)
-    sm_f[...] = jnp.zeros_like(sm_f)
-    sm_f[2 * N : 3 * N, :] = rate_sum * rate
+
+    def outputs(i, carry):
+        y = []
+        for k in range(CHUNK):
+            k = i * CHUNK + k
+            c_diag = (dot(ag1[tokens(k), R:], sel_c[...]) * dmask[...]).astype(BF16)
+            y.append(dot(c_diag, state_rows(k)))
+        at = tokens(i, CT)
+        y = jnp.concatenate(y, 0) + ds_ref[...] * u_bf[at, :].astype(F32)
+        zg_o[at, :] = (gz[at, :] * y).astype(BF16)
+        return carry
+
+    lax.fori_loop(0, NB // CHUNK, outputs, 0)
+
+    def rate_part(i, acc):
+        for j in range(UNROLL_F):
+            t = i * UNROLL_F + j
+            acc = acc + row(delta, t) * ha_buf[state_at(t), :].astype(F32)
+        return acc
+
+    sm_f[2 * N : 3 * N, :] = lax.fori_loop(0, T // UNROLL_F, rate_part, zero_state)
+    sm_f[3 * N :, :] = jnp.zeros((SM - 3 * N, C), F32)
     sm_f[3 * N + 5 : 3 * N + 6, :] = jnp.sum(pregrad[...], 0, keepdims=True)
-    sm_f[3 * N + 6 : 3 * N + 7, :] = jnp.sum(gy[...] * u32, 0, keepdims=True)
+    sm_f[3 * N + 6 : 3 * N + 7, :] = jnp.sum(gy[...] * u_bf[...].astype(F32), 0, keepdims=True)
 
     grad_rows = collect(chan(2), rs2, my_rows(part))
     low = low_own[...]
@@ -380,11 +438,13 @@
     spread(seq(1), dw_ag, RB)
 
     arrive(chan(3), ag2, ROWS)
-    keep = iota((T, W), 1) < R + 2 * N
-    pg = jnp.where(keep, ag2[...].astype(F32), 0.0).astype(BF16)
-    act = pre_act[...]
-    total = uscan[...] + dot(pg, xwp[...])
-    act_grad = total * silu_grad(act)
+
+    xl_f[...] = dot_tn(ag2[...], u_bf[...])
+    xl_send[...] = xl_f[:R, :].astype(BF16)
+    scatter(seq(2), xl_send, xl_rs, RB)
+    sm_f[: 2 * N, :] = xl_f[R:P2, :]
+    total = uscan[...] + dot(ag2[:, :R], xw_ref[:R, :]) + dot(ag2[:, R:P2], xw_ref[R:, :])
+    act_grad = total * act_slope[...]
     apad[:T, :] = act_grad
     apad[T:, :] = jnp.zeros((8, C), F32)
 
@@ -392,10 +452,6 @@
     def _():
         halo_copy(apad.at[:8, :], halo_a, 1, before).start()
 
-    xl_f[...] = dot_tn(pg, u_bf[...])
-    xl_send[...] = xl_f[:R, :].astype(BF16)
-    scatter(seq(2), xl_send, xl_rs, RB)
-    sm_f[: 2 * N, :] = xl_f[R : R + 2 * N, :]
     for k in range(4):
         sm_f[3 * N + k : 3 * N + k + 1, :] = jnp.sum(act_grad * xpad[5 + k : 5 + k + T, :], 0, keepdims=True)
     sm_f[3 * N + 4 : 3 * N + 5, :] = jnp.sum(act_grad, 0, keepdims=True)
@@ -492,8 +548,10 @@
 
     dma = pltpu.SemaphoreType.DMA
     scratch = dict(
-        xpad=f32(T + 8, C), pre_act=f32(T, C), u_bf=b16(T, C), gy=f32(T, C), gz=f32(T, C),
-        xwp=b16(W, C), part=f32(T, W), send1=b16(T, W), rs1=b16(NC, ROWS, W), ag1=b16(T, W),
+        x_ref=b16(T, C), z_ref=b16(T, C), g_ref=b16(T, C), cw_ref=f32(4, C), cb_ref=f32(1, C), xw_ref=b16(R + 2 * N, C),
+        dw_ref=b16(R, C), db_ref=f32(1, C), al_ref=f32(N, C), ds_ref=f32(1, C), dg_ref=f32(1, R),
+        xpad=f32(T + 8, C), pre_act=f32(T, C), act_slope=f32(T, C), u_bf=b16(T, C), gy=f32(T, C), gz=f32(T, C),
+        part=f32(T, W), send1=b16(T, W), rs1=b16(NC, ROWS, W), ag1=b16(T, W),
         low_own=f32(ROWS, R), inv_own=f32(ROWS, LANES),
         pre_soft=f32(T, C), delta=f32(T, C), drive=f32(T, C), bB=f32(T * N, LANES), cB=f32(T * N, LANES),
         a_buf=f32(T * N, C), h_buf=b16((T + 1) * N, C), lam_buf=b16(T * N, C), ha_buf=b16(T * N, C),
@@ -501,13 +559,13 @@
         in_tot=f32(NS, 1, C), carry_f=f32(N, C), carry_b=f32(N, C),
         e_exp=b16(GN, GROUP), m_b=f32(GN, LANES), m_c=f32(GN, LANES), sel_b=b16(LANES, GN), sel_c=b16(LANES, GN),
         dmask=f32(GROUP, GN), back_b=b16(GN, LANES), back_c=b16(GN, LANES),
-        yv=f32(T, C), bcg=f32(T, LANES), uscan=f32(T, C), pregrad=f32(T, C), prehalf=b16(T, C),
+        bcg=f32(T, LANES), uscan=f32(T, C), pregrad=f32(T, C), prehalf=b16(T, C),
         send2=b16(T, W), rs2=b16(NC, ROWS, W), ag2=b16(T, W),
         dw_f=f32(R, C), dw_send=b16(R, C), dw_rs=b16(NS, R // NS, C),
         xl_f=f32(W, C), xl_send=b16(R, C), xl_rs=b16(NS, R // NS, C),
         sm_f=f32(SM, C), sm_rs=f32(NS, SM // NS, C),
         halo_x=b16(16, C), halo_a=f32(8, C), apad=f32(T + 8, C),
-        s_c=dma((4, NC)), r_c=dma((4, NC)), s_st=dma((3, NS)), r_st=dma((3, NS)),
+        s_in=dma((11,)), s_c=dma((4, NC)), r_c=dma((4, NC)), s_st=dma((3, NS)), r_st=dma((3, NS)),
         s_sq=dma((6, NS)), r_sq=dma((6, NS)), s_h=dma((2,)), r_h=dma((2,)),
     )
     S = jax.ShapeDtypeStruct
@@ -515,7 +573,7 @@
     raw = pl.pallas_call(
         functools.partial(layer_kernel, dims),
         out_shape=(S((T, C), BF16), S((T, C), BF16), S((R, C), BF16), S((R, C), BF16), S((SM, C), F32)),
-        in_specs=[vmem] * 11,
+        in_specs=[pl.BlockSpec(memory_space=pl.ANY)] * 11,
         out_specs=(vmem,) * 5,
         scratch_shapes=list(scratch.values()),
         compiler_params=pltpu.CompilerParams(

time: 83 us -> 73.3 us (0.88)
  Pallas kernels: 82.2 us -> 72.5 us
    pallas_call x1, Pallas kernels: 79.8 us -> 70.1 us  [per_device(): pl.pallas_call(functools.partial(layer_kernel, dims), out_shape=(S((T, C)...]
where the time goes in v2:
time: 73.3 us; the launch traced here: 73.1 us
  Pallas kernels  72.5 us (99%)
    pallas_call x1, Pallas kernels, per_device(): pl.pallas_call(functools.partial(layer_kernel, dims), out_shape=(S((T, C)...  70.1 us
    pallas_call x1, Pallas kernels, per_device(): pl.pallas_call(functools.partial(finish_kernel, dims), out_shape=(S((T, C...  2.42 us

profile of v2, /device:TPU:1, one launch (start us, length us, event | category | flops | bytes accessed | tf_op | source)
XLA Modules:
  0.0 73.1 jit_solution(6040867851739111896)
XLA Ops:
  0.6 70.1 %shard_map.186 = (bf16[256,512]{1,0:T(8,128)(2,1)}, bf16[256,512]{1,0:T(8,128)(2,1)}, bf16[256,512]{1,0:T(8,128)(2,1)}, bf16[256,512]{1,0:T(8,128)(2,1)}, f32[64,512]{1,0:T(8,128)}) custom-call(bf16[256,512]{1,0:T(8,128)(2,1)} %refs_0_.1, bf16[256,512]{1,0:T(8,128)(2,1)} %refs_1_.1, bf16[256,512]{1,0:T(8,128)(2,1)} %refs_2_.1, f32[4,512]{1,0:T(4,128)} %refs_3_.1, ...), custom_call_target="tpu_custom_call" | custom-call | tf_op jit(solution)/shard_map/pallas_call | solution.py:573
  70.7 2.4 %shard_map.187 = (bf16[256,512]{1,0:T(8,128)(2,1)}, bf16[256,512]{1,0:T(8,128)(2,1)}, f32[4,512]{1,0:T(4,128)}, f32[1,512]{1,0:T(1,128)}, f32[288,512]{1,0:T(8,1...) custom-call(bf16[256,512]{1,0:T(8,128)(2,1)} %get-tuple-element.25.x, ...), custom_call_target="tpu_custom_call" | custom-call | tf_op jit(solution)/shard_map/pallas_call | solution.py:585

commit v3 on v2

--- a/solution.py
+++ b/solution.py
@@ -17,7 +17,6 @@
 MESH = pl.DeviceIdType.MESH
 VMEM_BYTES = 60 * 1024 * 1024
 CHUNK = 4
-UNROLL_FP = UNROLL_BP = UNROLL_F = UNROLL_B = 16
 
 
 def dot(a, b):
@@ -79,13 +78,16 @@
     (xg_o, zg_o, dw_ag, xl_ag, sm_ag,
      x_ref, z_ref, g_ref, cw_ref, cb_ref, xw_ref, dw_ref, db_ref, al_ref, ds_ref, dg_ref,
      xpad, pre_act, act_slope, u_bf, gy, gz, part, send1, rs1, ag1, low_own, inv_own,
-     pre_soft, delta, drive, bB, cB, a_buf, h_buf, lam_buf, ha_buf,
+     pre_soft, delta, drive, bB, cB, a_buf, h0, h1, lam0, lam1, ha0, ha1,
      st_f, st_b, tot, in_f, in_b, in_tot, carry_f, carry_b,
      e_exp, m_b, m_c, sel_b, sel_c, dmask, back_b, back_c,
-     bcg, uscan, pregrad, prehalf, send2, rs2, ag2,
-     dw_f, dw_send, dw_rs, xl_f, xl_send, xl_rs, sm_f, sm_rs,
+     b_diag, c_diag, b_all, c_all, adj_all, by_all, uscan, pregrad, prehalf, send2, rs2, ag2,
+     dw_f, dw_send, dw_rs, xl_f, xl_send, xl_rs, sm_f, sm_own, sm_send, sm_rs,
      halo_x, halo_a, apad,
      s_in, s_c, r_c, s_st, r_st, s_sq, r_sq, s_h, r_h) = refs
+    h_buf, lam_buf, ha_buf = (h0, h1), (lam0, lam1), (ha0, ha1)
+    HC = C // 2
+    HALVES = (slice(0, HC), slice(HC, C))
     ROWS = T // NC
     W = R + LANES
     P2 = R + 2 * N
@@ -93,7 +95,7 @@
     GN = GROUP * N
     RB = R // NS
     SM = sm_f.shape[0]
-    SB = SM // NS
+    SB = 2 * SM // NS
     ms, mc = lax.axis_index("seq"), lax.axis_index("chan")
 
     def chan(k):
@@ -209,7 +211,7 @@
     k_row, col_n = iota((LANES, GN), 0), iota((LANES, GN), 1) % N
     sel_b[...] = ((k_row == col_n) | (k_row == col_n + 2 * N)).astype(F32).astype(BF16)
     sel_c[...] = ((k_row == col_n + N) | (k_row == col_n + 3 * N)).astype(F32).astype(BF16)
-    dmask[...] = (iota((GROUP, GN), 1) // N == iota((GROUP, GN), 0)).astype(F32)
+    dmask[...] = (iota(dmask.shape, 1) // N == iota(dmask.shape, 0) % GROUP).astype(F32)
     rate = -jnp.exp(al_ref[...])
     rate2 = rate * LOG2E
 
@@ -228,8 +230,10 @@
     ag1[mine, :R] = (low * inv * dg_ref[...]).astype(BF16)
     ag1[mine, R:] = tail.astype(BF16)
     spread(chan(1), ag1, ROWS)
-    act_slope[...] = silu_grad(pre_act[...])
     arrive(chan(1), ag1, ROWS)
+
+    def tokens(i, count=GROUP):
+        return pl.ds(pl.multiple_of(i * count, count), count)
 
     soft = dot(ag1[:, :R], dw_ref[...]) + db_ref[...]
     pre_soft[...] = soft
@@ -240,137 +244,179 @@
     for peer in states(2).peers():
         states(2).send(tot, in_tot.at[ms], peer)
 
-    def tokens(i, count=GROUP):
-        return pl.ds(pl.multiple_of(i * count, count), count)
-
     ones = jnp.ones((LANES, LANES), BF16)
 
-    def widen(i, carry):
-        spread_rows = [dot(e_exp[...], ag1[tokens(i * CHUNK + k), R:]) for k in range(CHUNK)]
-        for k in range(CHUNK):
-            at = pl.ds(pl.multiple_of((i * CHUNK + k) * GN, GN), GN)
-            bB[at, :] = dot((spread_rows[k] * m_b[...]).astype(BF16), ones)
-            cB[at, :] = dot((spread_rows[k] * m_c[...]).astype(BF16), ones)
-        return carry
-
-    lax.fori_loop(0, NB // CHUNK, widen, 0)
-
-    def row(ref, t):
-        return ref[pl.ds(t, 1), :]
-
-    def state_at(t):
-        return pl.ds(pl.multiple_of(t * N, N), N)
-
-    def wide(ref, t):
-        return jnp.concatenate([ref[state_at(t), :]] * (C // LANES), axis=1)
+    def widen(out, mask):
+        def some(i, carry):
+            spread_rows = [dot(e_exp[...], ag1[tokens(i * CHUNK + k), R:]) for k in range(CHUNK)]
+            for k in range(CHUNK):
+                at = pl.ds(pl.multiple_of((i * CHUNK + k) * GN, GN), GN)
+                out[at, :] = dot((spread_rows[k] * mask[...]).astype(BF16), ones)
+            return carry
+
+        lax.fori_loop(0, NB // CHUNK, some, 0)
+
+    def rows_from(ref, first, count, sl=slice(None)):
+        return ref.at[pl.ds(pl.multiple_of(first, 8), count), sl]
+
+    def states_from(ref, first, count, sl=slice(None)):
+        return ref.at[pl.ds(pl.multiple_of(first * N, 8 * N), count * N), sl]
+
+    def row(view, j):
+        return view[j : j + 1, :]
+
+    def state(view, j):
+        return view[j * N : (j + 1) * N, :]
+
+    def wide(view, j, width):
+        return jnp.concatenate([view[j * N : (j + 1) * N, :]] * (width // LANES), axis=1)
 
     zero_state = jnp.zeros((N, C), F32)
+    rates = [rate[:, sl] for sl in HALVES]
 
     def forward_part(i, h):
-        for j in range(UNROLL_FP):
-            t = i * UNROLL_FP + j
-            a = jnp.exp2(row(delta, t) * rate2)
-            a_buf[state_at(t), :] = a
-            h = a * h + row(drive, t) * wide(bB, t)
+        first = i * GROUP
+        steps, drives = (rows_from(ref, first, GROUP) for ref in (delta, drive))
+        decays, b_rows = (states_from(ref, first, GROUP) for ref in (a_buf, bB))
+        for j in range(GROUP):
+            a = jnp.exp2(row(steps, j) * rate2)
+            decays[j * N : (j + 1) * N, :] = a
+            h = a * h + row(drives, j) * wide(b_rows, j, C)
         return h
 
-    st_f[...] = lax.fori_loop(0, T // UNROLL_FP, forward_part, zero_state).astype(BF16)
+    def backward_part(i, g):
+        first = T - GROUP * (i + 1)
+        grads = rows_from(gy, first, GROUP)
+        decays, c_rows = (states_from(ref, first, GROUP) for ref in (a_buf, cB))
+        for j in reversed(range(GROUP)):
+            g = state(decays, j) * (row(grads, j) * wide(c_rows, j, C) + g)
+        return g
+
+    def forward_carry():
+        for peer in states(2).peers():
+            states(2).wait_recv(in_tot.at[peer], peer)
+        carry_f[...] = zero_state
+        for s in range(NS - 1):
+
+            @pl.when(s < ms)
+            def _(s=s):
+                states(0).wait_recv(in_f.at[s], s)
+                carry_f[...] = jnp.exp2(in_tot[s] * rate2) * carry_f[...] + in_f[s].astype(F32)
+
+    def backward_carry():
+        carry_b[...] = zero_state
+        for s in range(NS - 1, 0, -1):
+
+            @pl.when(s > ms)
+            def _(s=s):
+                states(1).wait_recv(in_b.at[s], s)
+                carry_b[...] = jnp.exp2(in_tot[s] * rate2) * carry_b[...] + in_b[s].astype(F32)
+
+    def forward_block(hf, k, h):
+        first = k * GROUP
+        drives = rows_from(drive, first, GROUP, HALVES[hf])
+        decays, b_rows = states_from(a_buf, first, GROUP, HALVES[hf]), states_from(bB, first, GROUP)
+        later = h_buf[hf].at[pl.ds(pl.multiple_of(first * N + N, N), GROUP * N), :]
+        for j in range(GROUP):
+            h = state(decays, j) * h + row(drives, j) * wide(b_rows, j, HC)
+            later[j * N : (j + 1) * N, :] = h.astype(BF16)
+        return h
+
+    def start_states(hf):
+        start = carry_f[:, HALVES[hf]]
+        h_buf[hf][:N, :] = start.astype(BF16)
+        return start
+
+    def state_rows(hf, k):
+        return h_buf[hf][pl.ds(pl.multiple_of(k * GN + N, N), GN), :]
+
+    def adjoint_rows(buf, k):
+        return buf[pl.ds(pl.multiple_of(k * GN, GN), GN), :]
+
+    def backward_block(hf, k, g):
+        sl = HALVES[hf]
+        first = k * GROUP
+        grads = rows_from(gy, first, GROUP, sl)
+        befores, lams, has = (states_from(ref[hf], first, GROUP) for ref in (h_buf, lam_buf, ha_buf))
+        decays = states_from(a_buf, first, GROUP, sl)
+        c_rows = states_from(cB, first, GROUP)
+        for j in reversed(range(GROUP)):
+            lam = row(grads, j) * wide(c_rows, j, HC) + g
+            g = state(decays, j) * lam
+            hold = g * state(befores, j).astype(F32)
+            lams[j * N : (j + 1) * N, :] = lam.astype(BF16)
+            has[j * N : (j + 1) * N, :] = (hold * rates[hf]).astype(BF16)
+        return g
+
+    def state_sums(hf, k):
+        lam_rows = adjoint_rows(lam_buf[hf], k)
+        adj_b = dot(b_diag[tokens(k), :], lam_rows)
+        by_rate = dot(dmask[:GROUP, :].astype(BF16), adjoint_rows(ha_buf[hf], k))
+        return adj_b, by_rate, dot_nt(drive[tokens(k), HALVES[hf]].astype(BF16), lam_rows)
+
+    def c_sums(hf, k):
+        return dot_nt(gy[tokens(k), HALVES[hf]].astype(BF16), state_rows(hf, k))
+
+    def half_grads(hf, at, adj_b, by_rate):
+        sl = HALVES[hf]
+        pre = (by_rate + adj_b * u_bf[at, sl].astype(F32)) * jax.nn.sigmoid(pre_soft[at, sl])
+        pregrad[at, sl] = pre
+        prehalf[at, sl] = pre.astype(BF16)
+        uscan[at, sl] = ds_ref[:, sl] * gy[at, sl] + delta[at, sl] * adj_b
+
+    widen(bB, m_b)
+    st_f[...] = lax.fori_loop(0, NB, forward_part, zero_state).astype(BF16)
     for d in range(1, NS):
 
         @pl.when(ms + d < NS)
         def _(d=d):
             states(0).send(st_f, in_f.at[ms], ms + d)
 
-    def backward_part(i, g):
-        for j in range(UNROLL_BP):
-            t = T - 1 - (i * UNROLL_BP + j)
-            g = a_buf[state_at(t), :] * (row(gy, t) * wide(cB, t) + g)
-        return g
-
-    st_b[...] = lax.fori_loop(0, T // UNROLL_BP, backward_part, zero_state).astype(BF16)
+    widen(cB, m_c)
+    st_b[...] = lax.fori_loop(0, NB, backward_part, zero_state).astype(BF16)
     for d in range(1, NS):
 
         @pl.when(ms - d >= 0)
         def _(d=d):
             states(1).send(st_b, in_b.at[ms], ms - d)
 
-    for peer in states(2).peers():
-        states(2).wait_recv(in_tot.at[peer], peer)
-    carry_f[...] = zero_state
-    for s in range(NS - 1):
-
-        @pl.when(s < ms)
-        def _(s=s):
-            states(0).wait_recv(in_f.at[s], s)
-            carry_f[...] = jnp.exp2(in_tot[s] * rate2) * carry_f[...] + in_f[s].astype(F32)
-
-    start = carry_f[...]
-    h_buf[:N, :] = start.astype(BF16)
-
-    def forward(i, h):
-        for j in range(UNROLL_F):
-            t = i * UNROLL_F + j
-            h = a_buf[state_at(t), :] * h + row(drive, t) * wide(bB, t)
-            h_buf[state_at(t + 1), :] = h.astype(BF16)
-        return h
-
-    lax.fori_loop(0, T // UNROLL_F, forward, start)
-
-    def state_rows(k):
-        return h_buf[pl.ds(pl.multiple_of(k * GN + N, N), GN), :]
-
-    def after_forward(i, carry):
-        for k in range(CHUNK):
-            k = i * CHUNK + k
-            c_all = dot_nt(gy[tokens(k), :].astype(BF16), state_rows(k)) * dmask[...]
-            bcg[tokens(k), :] = dot(c_all.astype(BF16), back_c[...])
-        return carry
-
-    lax.fori_loop(0, NB // CHUNK, after_forward, 0)
-
-    carry_b[...] = zero_state
-    for s in range(NS - 1, 0, -1):
-
-        @pl.when(s > ms)
-        def _(s=s):
-            states(1).wait_recv(in_b.at[s], s)
-            carry_b[...] = jnp.exp2(in_tot[s] * rate2) * carry_b[...] + in_b[s].astype(F32)
-
+    act_slope[...] = silu_grad(pre_act[...])
+    mask = (iota((T, GN), 1) // N == iota((T, GN), 0) % GROUP).astype(F32)
+    b_diag[...] = (dot(ag1[:, R:], sel_b[...]) * mask).astype(BF16)
+    c_diag[...] = (dot(ag1[:, R:], sel_c[...]) * mask).astype(BF16)
+
+    def states_both(i, carry):
+        g, h = carry
+        c_all[tokens(i), :] = c_sums(0, i)
+        return backward_block(0, NB - 1 - i, g), forward_block(1, i, h)
+
+    forward_carry()
+    lax.fori_loop(0, NB, functools.partial(forward_block, 0), start_states(0))
+    backward_carry()
+    lax.fori_loop(0, NB, states_both, (carry_b[:, HALVES[0]], start_states(1)))
     CT = CHUNK * GROUP
 
     def backward_chunk(i, g):
         c = NB // CHUNK - 1 - i
 
-        def backward(m, g):
-            for j in range(UNROLL_B):
-                t = c * CT + CT - 1 - (m * UNROLL_B + j)
-                lam = row(gy, t) * wide(cB, t) + g
-                g = a_buf[state_at(t), :] * lam
-                hold = g * h_buf[state_at(t), :].astype(F32)
-                lam_buf[state_at(t), :] = lam.astype(BF16)
-                ha_buf[state_at(t), :] = (hold * rate).astype(BF16)
-            return g
-
-        g = lax.fori_loop(0, CT // UNROLL_B, backward, g)
+        def backward_second(m, g):
+            k = c * CHUNK + CHUNK - 1 - m
+            at = tokens(k)
+            adj_all[at, :], by_all[at, :], b_all[at, :] = state_sums(0, k)
+            c_all[at, :] = c_all[at, :] + c_sums(1, k)
+            return backward_block(1, k, g)
+
+        g = lax.fori_loop(0, CHUNK, backward_second, g)
         at = tokens(c, CT)
-        adj_b, by_rate, b_grad = [], [], []
-        for k in range(CHUNK):
-            k = c * CHUNK + k
-            states_k = pl.ds(pl.multiple_of(k * GN, GN), GN)
-            lam_rows = lam_buf[states_k, :]
-            b_diag = (dot(ag1[tokens(k), R:], sel_b[...]) * dmask[...]).astype(BF16)
-            adj_b.append(dot(b_diag, lam_rows))
-            by_rate.append(dot(dmask[...].astype(BF16), ha_buf[states_k, :]))
-            b_all = dot_nt(drive[tokens(k), :].astype(BF16), lam_rows) * dmask[...]
-            b_grad.append(dot(b_all.astype(BF16), back_b[...]))
-        adj_b = jnp.concatenate(adj_b, 0)
-        pre = (jnp.concatenate(by_rate, 0) + adj_b * u_bf[at, :].astype(F32)) * jax.nn.sigmoid(pre_soft[at, :])
-        pregrad[at, :] = pre
-        half = pre.astype(BF16)
-        prehalf[at, :] = half
-        uscan[at, :] = ds_ref[...] * gy[at, :] + delta[at, :] * adj_b
-        normed = dot_nt(half, dw_ref[...])
-        tail = bcg[at, :] + jnp.concatenate(b_grad, 0)
+        sums = [state_sums(1, c * CHUNK + k) for k in range(CHUNK)]
+        half_grads(0, at, adj_all[at, :], by_all[at, :])
+        b_cols = (c_all[at, :] * dmask[...]).astype(BF16)
+        tail = dot(b_cols, back_c[...])
+        adj_b, by_rate, b_sums = (jnp.concatenate(parts, 0) for parts in zip(*sums))
+        half_grads(1, at, adj_b, by_rate)
+        b_cols = ((b_all[at, :] + b_sums) * dmask[...]).astype(BF16)
+        tail = tail + dot(b_cols, back_b[...])
+        normed = dot_nt(prehalf[at, :], dw_ref[...])
         part[at, :R] = normed
         part[at, R:] = tail
         send2[at, :R] = normed.astype(BF16)
@@ -384,7 +430,7 @@
 
         return g
 
-    lax.fori_loop(0, NB // CHUNK, backward_chunk, carry_b[...])
+    lax.fori_loop(0, NB // CHUNK, backward_chunk, carry_b[:, HALVES[1]])
 
     dw_f[...] = dot_tn(ag1[:, :R], prehalf[...])
     dw_send[...] = dw_f[...].astype(BF16)
@@ -394,8 +440,7 @@
         y = []
         for k in range(CHUNK):
             k = i * CHUNK + k
-            c_diag = (dot(ag1[tokens(k), R:], sel_c[...]) * dmask[...]).astype(BF16)
-            y.append(dot(c_diag, state_rows(k)))
+            y.append(jnp.concatenate([dot(c_diag[tokens(k), :], state_rows(hf, k)) for hf in range(2)], 1))
         at = tokens(i, CT)
         y = jnp.concatenate(y, 0) + ds_ref[...] * u_bf[at, :].astype(F32)
         zg_o[at, :] = (gz[at, :] * y).astype(BF16)
@@ -403,13 +448,16 @@
 
     lax.fori_loop(0, NB // CHUNK, outputs, 0)
 
-    def rate_part(i, acc):
-        for j in range(UNROLL_F):
-            t = i * UNROLL_F + j
-            acc = acc + row(delta, t) * ha_buf[state_at(t), :].astype(F32)
-        return acc
-
-    sm_f[2 * N : 3 * N, :] = lax.fori_loop(0, T // UNROLL_F, rate_part, zero_state)
+    for hf in range(2):
+
+        def rate_part(i, acc):
+            steps = rows_from(delta, i * GROUP, GROUP, HALVES[hf])
+            has = states_from(ha_buf[hf], i * GROUP, GROUP)
+            for j in range(GROUP):
+                acc = acc + row(steps, j) * state(has, j).astype(F32)
+            return acc
+
+        sm_f[2 * N : 3 * N, HALVES[hf]] = lax.fori_loop(0, NB, rate_part, zero_state[:, :HC])
     sm_f[3 * N :, :] = jnp.zeros((SM - 3 * N, C), F32)
     sm_f[3 * N + 5 : 3 * N + 6, :] = jnp.sum(pregrad[...], 0, keepdims=True)
     sm_f[3 * N + 6 : 3 * N + 7, :] = jnp.sum(gy[...] * u_bf[...].astype(F32), 0, keepdims=True)
@@ -464,7 +512,10 @@
         sm_f[3 * N + 7 : 3 * N + 8, k * LANES : (k + 1) * LANES] = jnp.where(
             low_half, pltpu.roll(gq[2 * k : 2 * k + 1], half, 1), gq[2 * k + 1 : 2 * k + 2]
         )
-    scatter(seq(3), sm_f, sm_rs, SB)
+    for k in range(2):
+        sm_own[k * SM : (k + 1) * SM, :] = sm_f[:, k * HC : (k + 1) * HC]
+    sm_send[...] = sm_own[...].astype(BF16)
+    scatter(seq(3), sm_send, sm_rs, SB)
 
     @pl.when(ms < NS - 1)
     def _():
@@ -480,7 +531,7 @@
     xl_ag[at, :] = collect(seq(2), xl_rs, xl_f[at, :]).astype(BF16)
     spread(seq(4), xl_ag, RB)
     at = pl.ds(pl.multiple_of(ms * SB, SB), SB)
-    sm_ag[at, :] = collect(seq(3), sm_rs, sm_f[at, :])
+    sm_ag[at, :] = collect(seq(3), sm_rs, sm_own[at, :]).astype(BF16)
     spread(seq(5), sm_ag, SB)
     arrive(seq(1), dw_ag, RB)
     arrive(seq(4), xl_ag, RB)
@@ -489,7 +540,7 @@
     for k, size, src in ((0, ROWS, send1), (1, ROWS, ag1), (2, ROWS, send2), (3, ROWS, ag2)):
         for peer in chan(k).peers():
             chan(k).wait_send(src.at[:size, :], peer)
-    for k, size, src in ((0, RB, dw_send), (1, RB, dw_ag), (2, RB, xl_send), (3, SB, sm_f), (4, RB, xl_ag), (5, SB, sm_ag)):
+    for k, size, src in ((0, RB, dw_send), (1, RB, dw_ag), (2, RB, xl_send), (3, SB, sm_send), (4, RB, xl_ag), (5, SB, sm_ag)):
         for peer in seq(k).peers():
             seq(k).wait_send(src.at[:size, :], peer)
     for peer in states(2).peers():
@@ -520,13 +571,19 @@
     zg_o[...] = zg[...]
     dwg_o[...] = scale * dw_sum[...].astype(F32)
     xpg_o[:R, :] = scale * xl_sum[...].astype(F32)
-    xpg_o[R:, :] = scale * sm_sum[: 2 * N, :]
-    alg_o[...] = scale * sm_sum[2 * N : 3 * N, :]
-    cwg_o[...] = scale * sm_sum[3 * N : 3 * N + 4, :]
-    cbg_o[...] = scale * sm_sum[3 * N + 4 : 3 * N + 5, :]
-    dbg_o[...] = scale * sm_sum[3 * N + 5 : 3 * N + 6, :]
-    dsg_o[...] = scale * sm_sum[3 * N + 6 : 3 * N + 7, :]
-    dgg_o[...] = scale * sm_sum[3 * N + 7 : 3 * N + 8, :R]
+    HC = C // 2
+    small = scale * sm_sum[...].astype(F32)
+    for hf in range(2):
+        sl = slice(hf * HC, (hf + 1) * HC)
+        rows = small[hf * 4 * N : (hf + 1) * 4 * N]
+        xpg_o[R:, sl] = rows[: 2 * N]
+        alg_o[:, sl] = rows[2 * N : 3 * N]
+        cwg_o[:, sl] = rows[3 * N : 3 * N + 4]
+        cbg_o[:, sl] = rows[3 * N + 4 : 3 * N + 5]
+        dbg_o[:, sl] = rows[3 * N + 5 : 3 * N + 6]
+        dsg_o[:, sl] = rows[3 * N + 6 : 3 * N + 7]
+        if hf * HC < R:
+            dgg_o[:, sl] = rows[3 * N + 7 : 3 * N + 8]
 
 
 def per_device(counts, x_in, z_in, grad_out, conv_w, conv_b, xproj_w, dt_w, dt_bias, a_log, d_skip, dt_gain):
@@ -538,6 +595,7 @@
     W = R + LANES
     GN = GROUP * N
     SM = 4 * N
+    HC = C // 2
     dims = (T, C, NS, NC, R, N)
 
     def f32(*shape):
@@ -554,16 +612,18 @@
         part=f32(T, W), send1=b16(T, W), rs1=b16(NC, ROWS, W), ag1=b16(T, W),
         low_own=f32(ROWS, R), inv_own=f32(ROWS, LANES),
         pre_soft=f32(T, C), delta=f32(T, C), drive=f32(T, C), bB=f32(T * N, LANES), cB=f32(T * N, LANES),
-        a_buf=f32(T * N, C), h_buf=b16((T + 1) * N, C), lam_buf=b16(T * N, C), ha_buf=b16(T * N, C),
+        a_buf=f32(T * N, C), h0=b16((T + 1) * N, HC), h1=b16((T + 1) * N, HC),
+        lam0=b16(T * N, HC), lam1=b16(T * N, HC), ha0=b16(T * N, HC), ha1=b16(T * N, HC),
         st_f=b16(N, C), st_b=b16(N, C), tot=f32(1, C), in_f=b16(NS, N, C), in_b=b16(NS, N, C),
         in_tot=f32(NS, 1, C), carry_f=f32(N, C), carry_b=f32(N, C),
         e_exp=b16(GN, GROUP), m_b=f32(GN, LANES), m_c=f32(GN, LANES), sel_b=b16(LANES, GN), sel_c=b16(LANES, GN),
-        dmask=f32(GROUP, GN), back_b=b16(GN, LANES), back_c=b16(GN, LANES),
-        bcg=f32(T, LANES), uscan=f32(T, C), pregrad=f32(T, C), prehalf=b16(T, C),
+        dmask=f32(CHUNK * GROUP, GN), back_b=b16(GN, LANES), back_c=b16(GN, LANES),
+        b_diag=b16(T, GN), c_diag=b16(T, GN), b_all=f32(T, GN), c_all=f32(T, GN), adj_all=f32(T, HC), by_all=f32(T, HC),
+        uscan=f32(T, C), pregrad=f32(T, C), prehalf=b16(T, C),
         send2=b16(T, W), rs2=b16(NC, ROWS, W), ag2=b16(T, W),
         dw_f=f32(R, C), dw_send=b16(R, C), dw_rs=b16(NS, R // NS, C),
         xl_f=f32(W, C), xl_send=b16(R, C), xl_rs=b16(NS, R // NS, C),
-        sm_f=f32(SM, C), sm_rs=f32(NS, SM // NS, C),
+        sm_f=f32(SM, C), sm_own=f32(2 * SM, HC), sm_send=b16(2 * SM, HC), sm_rs=b16(NS, 2 * SM // NS, HC),
         halo_x=b16(16, C), halo_a=f32(8, C), apad=f32(T + 8, C),
         s_in=dma((11,)), s_c=dma((4, NC)), r_c=dma((4, NC)), s_st=dma((3, NS)), r_st=dma((3, NS)),
         s_sq=dma((6, NS)), r_sq=dma((6, NS)), s_h=dma((2,)), r_h=dma((2,)),
@@ -572,7 +632,7 @@
     vmem = pl.BlockSpec(memory_space=pltpu.VMEM)
     raw = pl.pallas_call(
         functools.partial(layer_kernel, dims),
-        out_shape=(S((T, C), BF16), S((T, C), BF16), S((R, C), BF16), S((R, C), BF16), S((SM, C), F32)),
+        out_shape=(S((T, C), BF16), S((T, C), BF16), S((R, C), BF16), S((R, C), BF16), S((2 * SM, HC), BF16)),
         in_specs=[pl.BlockSpec(memory_space=pl.ANY)] * 11,
         out_specs=(vmem,) * 5,
         scratch_shapes=list(scratch.values()),

time: 73.3 us -> 67.8 us (0.925)
  Pallas kernels: 72.5 us -> 67 us
    pallas_call x1, Pallas kernels: 70.1 us -> 64.6 us  [per_device(): pl.pallas_call(functools.partial(layer_kernel, dims), out_shape=(S((T, C)...]
where the time goes in v3:
time: 67.8 us; the launch traced here: 67.6 us
  Pallas kernels  67 us (99%)
    pallas_call x1, Pallas kernels, per_device(): pl.pallas_call(functools.partial(layer_kernel, dims), out_shape=(S((T, C)...  64.6 us
    pallas_call x1, Pallas kernels, per_device(): pl.pallas_call(functools.partial(finish_kernel, dims), out_shape=(S((T, C...  2.41 us

profile of v3, /device:TPU:1, one launch (start us, length us, event | category | flops | bytes accessed | tf_op | source)
XLA Modules:
  0.0 67.6 jit_solution(3674506789868864940)
XLA Ops:
  0.6 64.6 %shard_map.186 = (bf16[256,512]{1,0:T(8,128)(2,1)}, bf16[256,512]{1,0:T(8,128)(2,1)}, bf16[256,512]{1,0:T(8,128)(2,1)}, bf16[256,512]{1,0:T(8,128)(2,1)}, bf16[128,256]{1,0:T(8,128)(2,1)}) custom-call(bf16[256,512]{1,0:T(8,128)(2,1)} %refs_0_.1, bf16[256,512]{1,0:T(8,128)(2,1)} %refs_1_.1, bf16[256,512]{1,0:T(8,128)(2,1)} %refs_2_.1, f32[4,512]{1,0:T(4,128)} %refs_3_.1, ...), custom_call_target="tpu_custom_call" | custom-call | tf_op jit(solution)/shard_map/pallas_call | solution.py:633
  65.2 2.4 %shard_map.187 = (bf16[256,512]{1,0:T(8,128)(2,1)}, bf16[256,512]{1,0:T(8,128)(2,1)}, f32[4,512]{1,0:T(4,128)}, f32[1,512]{1,0:T(1,128)}, f32[288,512]{1,0:T(8,1...) custom-call(bf16[256,512]{1,0:T(8,128)(2,1)} %get-tuple-element.25.x, ...), custom_call_target="tpu_custom_call" | custom-call | tf_op jit(solution)/shard_map/pallas_call | solution.py:645

commit v4 on v3

--- a/solution.py
+++ b/solution.py
@@ -60,7 +60,14 @@
         )
 
     def peers(self):
-        return [lax.rem(self.me + d, self.count) for d in range(1, self.count)]
+        minor = 4 if self.axis == "chan" else 2
+        major = self.count // minor
+        steps = [(a, b) for a in range(major) for b in range(minor) if (a, b) != (0, 0)]
+        steps.sort(key=lambda s: -min(s[0], major - s[0]) - min(s[1], minor - s[1]))
+        return [
+            lax.rem(self.me // minor + a, major) * minor + lax.rem(lax.rem(self.me, minor) + b, minor)
+            for a, b in steps
+        ]
 
     def send(self, src, dst, peer):
         self._copy(src, dst, peer, self.me, peer).start()
@@ -75,16 +82,16 @@
 def layer_kernel(dims, *refs):
     T, C, NS, NC, R, N = dims
     hbm, refs = refs[:11], refs[11:]
-    (xg_o, zg_o, dw_ag, xl_ag, sm_ag,
+    (xg_o, zg_o, dw_o, xl_ag, sm_ag,
      x_ref, z_ref, g_ref, cw_ref, cb_ref, xw_ref, dw_ref, db_ref, al_ref, ds_ref, dg_ref,
-     xpad, pre_act, act_slope, u_bf, gy, gz, part, send1, rs1, ag1, low_own, inv_own,
+     xg_v, zg_v, dw_ag, shifts, shifted, first_parts, pre_act, act_slope, u_bf, gy, gz, part, send1, rs1, ag1, low_own, inv_own,
      pre_soft, delta, drive, bB, cB, a_buf, h0, h1, lam0, lam1, ha0, ha1,
      st_f, st_b, tot, in_f, in_b, in_tot, carry_f, carry_b,
      e_exp, m_b, m_c, sel_b, sel_c, dmask, back_b, back_c,
-     b_diag, c_diag, b_all, c_all, adj_all, by_all, uscan, pregrad, prehalf, send2, rs2, ag2,
+     tail32, b_diag, c_diag, b_all, c_all, adj_all, by_all, uscan, pregrad, prehalf, send2, rs2, ag2,
      dw_f, dw_send, dw_rs, xl_f, xl_send, xl_rs, sm_f, sm_own, sm_send, sm_rs,
      halo_x, halo_a, apad,
-     s_in, s_c, r_c, s_st, r_st, s_sq, r_sq, s_h, r_h) = refs
+     s_in, s_out, s_c, r_c, s_st, r_st, s_sq, r_sq, s_h, r_h) = refs
     h_buf, lam_buf, ha_buf = (h0, h1), (lam0, lam1), (ha0, ha1)
     HC = C // 2
     HALVES = (slice(0, HC), slice(HC, C))
@@ -108,27 +115,31 @@
         return Exchange("seq", NS, ms, s_st.at[k], r_st.at[k])
 
     barrier = pltpu.get_barrier_semaphore()
-    for d in range(1, NC):
-        pl.semaphore_signal(barrier, inc=1, device_id={"chan": lax.rem(mc + d, NC)}, device_id_type=MESH)
-    for d in range(1, NS):
-        pl.semaphore_signal(barrier, inc=1, device_id={"seq": lax.rem(ms + d, NS)}, device_id_type=MESH)
+    for peer in chan(0).peers():
+        pl.semaphore_signal(barrier, inc=1, device_id={"chan": peer}, device_id_type=MESH)
+    for peer in seq(0).peers():
+        pl.semaphore_signal(barrier, inc=1, device_id={"seq": peer}, device_id_type=MESH)
     local = (x_ref, z_ref, g_ref, cw_ref, cb_ref, xw_ref, dw_ref, db_ref, al_ref, ds_ref, dg_ref)
     fetch = [pltpu.make_async_copy(hbm[k], local[k], s_in.at[k]) for k in range(11)]
     for k in (0, 3, 4, 5, 1, 2, 6, 7, 8, 9, 10):
         fetch[k].start()
 
-    xpad[:8, :] = jnp.zeros((8, C), F32)
+    for k in range(3):
+        shifts[k * T : (k + 1) * T, :] = (iota((T, T), 1) == iota((T, T), 0) + (k - 3)).astype(F32).astype(BF16)
+    part[:, R:] = jnp.zeros((T, LANES), F32)
+    send1[:, R:] = jnp.zeros((T, LANES), BF16)
     for k in (0, 3, 4):
         fetch[k].wait()
-    xpad[8:, :] = x_ref[...].astype(F32)
     cw = cw_ref[...]
+    shifted[...] = dot(shifts[...], x_ref[...]).astype(BF16)
 
     def conv(first, count):
-        total = jnp.broadcast_to(cb_ref[...], (count, C))
-        for k in range(4):
-            total = total + cw[k : k + 1] * xpad[first + 5 + k : first + 5 + k + count, :]
-        pre_act[first : first + count, :] = total
-        u_bf[first : first + count, :] = (total * jax.nn.sigmoid(total)).astype(BF16)
+        for r in range(first, first + count, 16):
+            total = cb_ref[...] + cw[3:4] * x_ref[r : r + 16, :].astype(F32)
+            for k in range(3):
+                total = total + cw[k : k + 1] * shifted[k * T + r : k * T + r + 16, :].astype(F32)
+            pre_act[r : r + 16, :] = total
+            u_bf[r : r + 16, :] = (total * jax.nn.sigmoid(total)).astype(BF16)
 
     def project(first, count):
         sums = dot_nt(u_bf[first : first + count, :], xw_ref[...])
@@ -137,6 +148,10 @@
         send1[first : first + count, :R] = sums[:, :R].astype(BF16)
         send1[first : first + count, R:P2] = sums[:, R:P2].astype(BF16)
 
+    conv(ROWS, T - ROWS)
+    fetch[5].wait()
+    project(ROWS, T - ROWS)
+
     def halo_copy(src, dst, k, peer):
         return pltpu.make_async_remote_copy(
             src_ref=src, dst_ref=dst, send_sem=s_h.at[k], recv_sem=r_h.at[k],
@@ -172,28 +187,11 @@
     def _():
         halo_copy(x_ref.at[T - 16 :, :], halo_x, 0, after).start()
 
-    part[:, R:] = jnp.zeros((T, LANES), F32)
-    send1[:, R:] = jnp.zeros((T, LANES), BF16)
-    conv(0, T)
-    fetch[5].wait()
-    project(ROWS, T - ROWS)
     for peer in chan(0).peers():
 
         @pl.when(peer != 0)
         def _(peer=peer):
             chan(0).send(block(send1, peer, ROWS), rs1.at[mc], peer)
-
-    @pl.when(ms > 0)
-    def _():
-        halo_copy(halo_x, halo_x, 0, before).wait_recv()
-        xpad[:8, :] = halo_x[...].astype(F32)[8:16]
-        conv(0, 16)
-
-    project(0, ROWS)
-
-    @pl.when(mc != 0)
-    def _():
-        chan(0).send(block(send1, 0, ROWS), rs1.at[mc], 0)
 
     for k in (1, 2, 6, 7, 8, 9, 10):
         fetch[k].wait()
@@ -215,43 +213,91 @@
     rate = -jnp.exp(al_ref[...])
     rate2 = rate * LOG2E
 
+    @pl.when(ms == 0)
+    def _():
+        halo_x[...] = jnp.zeros_like(halo_x)
+
+    @pl.when(ms > 0)
+    def _():
+        halo_copy(halo_x, halo_x, 0, before).wait_recv()
+
+    window = jnp.concatenate([halo_x[...], x_ref[:16, :]], 0)
+    near = iota((48, 32), 0)
+    near = (iota((48, 32), 1) == near % 16 + near // 16 + 13).astype(F32).astype(BF16)
+    near = dot(near, window).astype(BF16)
+    for k in range(3):
+        shifted[k * T : k * T + 16, :] = near[16 * k : 16 * k + 16]
+    conv(0, ROWS)
+    project(0, ROWS)
+    first_parts[mc] = send1[:ROWS, :]
+    for peer in chan(4).peers():
+        chan(4).send(first_parts.at[mc], first_parts.at[mc], peer)
+
+    mine = pl.ds(pl.multiple_of(mc * ROWS, ROWS), ROWS)
+
     def my_rows(ref):
-        return ref[pl.ds(pl.multiple_of(mc * ROWS, ROWS), ROWS), :]
-
-    proj = collect(chan(0), rs1, my_rows(part))
-    low = proj[:, :R]
-    inv = lax.rsqrt(jnp.mean(low * low, -1, keepdims=True) + EPS)
-    low_own[...] = low
-    inv_own[...] = jnp.broadcast_to(inv, inv_own.shape)
-    tail = proj[:, R:]
-    tail_hi = tail.astype(BF16).astype(F32)
-    tail = tail_hi + pltpu.roll(tail - tail_hi, 2 * N, 1)
-    mine = pl.ds(pl.multiple_of(mc * ROWS, ROWS), ROWS)
-    ag1[mine, :R] = (low * inv * dg_ref[...]).astype(BF16)
-    ag1[mine, R:] = tail.astype(BF16)
-    spread(chan(1), ag1, ROWS)
-    arrive(chan(1), ag1, ROWS)
+        return ref[mine, :]
+
+    def normed_rows(proj):
+        low = proj[:, :R]
+        inv = lax.rsqrt(jnp.mean(low * low, -1, keepdims=True) + EPS)
+        tail = proj[:, R:]
+        tail_hi = tail.astype(BF16).astype(F32)
+        tail = tail_hi + pltpu.roll(tail - tail_hi, 2 * N, 1)
+        return low, inv, (low * inv * dg_ref[...]).astype(BF16), tail.astype(BF16)
+
+    def keep(low, inv):
+        low_own[...] = low
+        inv_own[...] = jnp.broadcast_to(inv, inv_own.shape)
+
+    @pl.when(mc != 0)
+    def _():
+        low, inv, ag1[mine, :R], ag1[mine, R:] = normed_rows(collect(chan(0), rs1, my_rows(part)))
+        spread(chan(1), ag1, ROWS)
+        keep(low, inv)
+
+    for peer in chan(4).peers():
+        chan(4).wait_recv(first_parts.at[peer], peer)
+    proj = jnp.zeros((ROWS, W), F32)
+    for c in range(NC):
+        proj = proj + first_parts[c].astype(F32)
+    low, inv, ag1[:ROWS, :R], ag1[:ROWS, R:] = normed_rows(proj)
+
+    @pl.when(mc == 0)
+    def _():
+        keep(low, inv)
+
+    for peer in chan(1).peers():
+
+        @pl.when(peer != 0)
+        def _(peer=peer):
+            chan(1).wait_recv(block(ag1, peer, ROWS), peer)
 
     def tokens(i, count=GROUP):
         return pl.ds(pl.multiple_of(i * count, count), count)
 
-    soft = dot(ag1[:, :R], dw_ref[...]) + db_ref[...]
-    pre_soft[...] = soft
-    step = softplus(soft)
-    delta[...] = step
-    drive[...] = step * u_bf[...].astype(F32)
-    tot[...] = jnp.sum(step, 0, keepdims=True)
+    pre_soft[...] = dot(ag1[:, :R], dw_ref[...])
+    steps_sum = jnp.zeros((16, C), F32)
+    for r in range(0, T, 16):
+        soft = pre_soft[r : r + 16, :] + db_ref[...]
+        pre_soft[r : r + 16, :] = soft
+        step = softplus(soft)
+        delta[r : r + 16, :] = step
+        drive[r : r + 16, :] = step * u_bf[r : r + 16, :].astype(F32)
+        steps_sum = steps_sum + step
+    tot[...] = jnp.sum(steps_sum, 0, keepdims=True)
     for peer in states(2).peers():
         states(2).send(tot, in_tot.at[ms], peer)
 
     ones = jnp.ones((LANES, LANES), BF16)
 
+    tail32[...] = ag1[:, R:].astype(F32)
+
     def widen(out, mask):
         def some(i, carry):
-            spread_rows = [dot(e_exp[...], ag1[tokens(i * CHUNK + k), R:]) for k in range(CHUNK)]
-            for k in range(CHUNK):
-                at = pl.ds(pl.multiple_of((i * CHUNK + k) * GN, GN), GN)
-                out[at, :] = dot((spread_rows[k] * mask[...]).astype(BF16), ones)
+            rows = tail32.at[tokens(i, CHUNK * GROUP), :]
+            spread_rows = [(rows[j : j + 1, :] * mask[:N, :]).astype(BF16) for j in range(CHUNK * GROUP)]
+            out[pl.ds(pl.multiple_of(i * CHUNK * GN, GN), CHUNK * GN), :] = dot(jnp.concatenate(spread_rows, 0), ones)
             return carry
 
         lax.fori_loop(0, NB // CHUNK, some, 0)
@@ -366,7 +412,7 @@
 
     widen(bB, m_b)
     st_f[...] = lax.fori_loop(0, NB, forward_part, zero_state).astype(BF16)
-    for d in range(1, NS):
+    for d in range(NS - 1, 0, -1):
 
         @pl.when(ms + d < NS)
         def _(d=d):
@@ -374,7 +420,7 @@
 
     widen(cB, m_c)
     st_b[...] = lax.fori_loop(0, NB, backward_part, zero_state).astype(BF16)
-    for d in range(1, NS):
+    for d in range(NS - 1, 0, -1):
 
         @pl.when(ms - d >= 0)
         def _(d=d):
@@ -387,13 +433,16 @@
 
     def states_both(i, carry):
         g, h = carry
-        c_all[tokens(i), :] = c_sums(0, i)
-        return backward_block(0, NB - 1 - i, g), forward_block(1, i, h)
+        for k in range(2):
+            k = 2 * i + k
+            c_all[tokens(k), :] = c_sums(0, k)
+            g, h = backward_block(0, NB - 1 - k, g), forward_block(1, k, h)
+        return g, h
 
     forward_carry()
     lax.fori_loop(0, NB, functools.partial(forward_block, 0), start_states(0))
     backward_carry()
-    lax.fori_loop(0, NB, states_both, (carry_b[:, HALVES[0]], start_states(1)))
+    lax.fori_loop(0, NB // 2, states_both, (carry_b[:, HALVES[0]], start_states(1)))
     CT = CHUNK * GROUP
 
     def backward_chunk(i, g):
@@ -406,7 +455,8 @@
             c_all[at, :] = c_all[at, :] + c_sums(1, k)
             return backward_block(1, k, g)
 
-        g = lax.fori_loop(0, CHUNK, backward_second, g)
+        for m in range(CHUNK):
+            g = backward_second(m, g)
         at = tokens(c, CT)
         sums = [state_sums(1, c * CHUNK + k) for k in range(CHUNK)]
         half_grads(0, at, adj_all[at, :], by_all[at, :])
@@ -443,10 +493,12 @@
             y.append(jnp.concatenate([dot(c_diag[tokens(k), :], state_rows(hf, k)) for hf in range(2)], 1))
         at = tokens(i, CT)
         y = jnp.concatenate(y, 0) + ds_ref[...] * u_bf[at, :].astype(F32)
-        zg_o[at, :] = (gz[at, :] * y).astype(BF16)
+        zg_v[at, :] = (gz[at, :] * y).astype(BF16)
         return carry
 
     lax.fori_loop(0, NB // CHUNK, outputs, 0)
+    leave = [pltpu.make_async_copy(v, o, s_out.at[k]) for k, (v, o) in enumerate(((zg_v, zg_o), (xg_v, xg_o), (dw_ag, dw_o)))]
+    leave[0].start()
 
     for hf in range(2):
 
@@ -487,22 +539,34 @@
 
     arrive(chan(3), ag2, ROWS)
 
+    PB = RB // 2
+
+    def piece(ref, i, p):
+        return ref.at[pl.ds(pl.multiple_of(i * RB + p * PB, PB), PB), :]
+
     xl_f[...] = dot_tn(ag2[...], u_bf[...])
     xl_send[...] = xl_f[:R, :].astype(BF16)
-    scatter(seq(2), xl_send, xl_rs, RB)
+    for p in range(2):
+        for peer in seq(2 + p).peers():
+            seq(2 + p).send(piece(xl_send, peer, p), xl_rs.at[p, ms], peer)
     sm_f[: 2 * N, :] = xl_f[R:P2, :]
     total = uscan[...] + dot(ag2[:, :R], xw_ref[:R, :]) + dot(ag2[:, R:P2], xw_ref[R:, :])
-    act_grad = total * act_slope[...]
-    apad[:T, :] = act_grad
+    apad[:T, :] = total * act_slope[...]
     apad[T:, :] = jnp.zeros((8, C), F32)
 
     @pl.when(ms > 0)
     def _():
         halo_copy(apad.at[:8, :], halo_a, 1, before).start()
 
-    for k in range(4):
-        sm_f[3 * N + k : 3 * N + k + 1, :] = jnp.sum(act_grad * xpad[5 + k : 5 + k + T, :], 0, keepdims=True)
-    sm_f[3 * N + 4 : 3 * N + 5, :] = jnp.sum(act_grad, 0, keepdims=True)
+    sums = [jnp.zeros((16, C), F32) for _ in range(5)]
+    for r in range(0, T, 16):
+        grad = apad[r : r + 16, :]
+        for k in range(3):
+            sums[k] = sums[k] + grad * shifted[k * T + r : k * T + r + 16, :].astype(F32)
+        sums[3] = sums[3] + grad * x_ref[r : r + 16, :].astype(F32)
+        sums[4] = sums[4] + grad
+    for k in range(5):
+        sm_f[3 * N + k : 3 * N + k + 1, :] = jnp.sum(sums[k], 0, keepdims=True)
     g_sum = jnp.zeros((ROWS, LANES), F32)
     for c in range(NC):
         g_sum = g_sum + ag2[c * ROWS : (c + 1) * ROWS, R:].astype(F32)
@@ -515,34 +579,33 @@
     for k in range(2):
         sm_own[k * SM : (k + 1) * SM, :] = sm_f[:, k * HC : (k + 1) * HC]
     sm_send[...] = sm_own[...].astype(BF16)
-    scatter(seq(3), sm_send, sm_rs, SB)
+    scatter(seq(4), sm_send, sm_rs, SB)
 
     @pl.when(ms < NS - 1)
     def _():
         halo_copy(halo_a, halo_a, 1, after).wait_recv()
         apad[T:, :] = halo_a[...]
 
-    total = jnp.zeros((T, C), F32)
-    for k in range(4):
-        total = total + cw[k : k + 1] * apad[3 - k : 3 - k + T, :]
-    xg_o[...] = total.astype(BF16)
-
-    at = pl.ds(pl.multiple_of(ms * RB, RB), RB)
-    xl_ag[at, :] = collect(seq(2), xl_rs, xl_f[at, :]).astype(BF16)
-    spread(seq(4), xl_ag, RB)
-    at = pl.ds(pl.multiple_of(ms * SB, SB), SB)
-    sm_ag[at, :] = collect(seq(3), sm_rs, sm_own[at, :]).astype(BF16)
-    spread(seq(5), sm_ag, SB)
+    for r in range(0, T, 32):
+        total = cw[3:4] * apad[r : r + 32, :]
+        for k in range(3):
+            total = total + cw[k : k + 1] * apad[r + 3 - k : r + 3 - k + 32, :]
+        xg_v[r : r + 32, :] = total.astype(BF16)
+    leave[1].start()
     arrive(seq(1), dw_ag, RB)
-    arrive(seq(4), xl_ag, RB)
-    arrive(seq(5), sm_ag, SB)
-
-    for k, size, src in ((0, ROWS, send1), (1, ROWS, ag1), (2, ROWS, send2), (3, ROWS, ag2)):
+    leave[2].start()
+
+    for k, size, src in ((0, ROWS, send1), (1, ROWS, ag1), (2, ROWS, send2), (3, ROWS, ag2), (4, ROWS, send1)):
         for peer in chan(k).peers():
-            chan(k).wait_send(src.at[:size, :], peer)
-    for k, size, src in ((0, RB, dw_send), (1, RB, dw_ag), (2, RB, xl_send), (3, SB, sm_send), (4, RB, xl_ag), (5, SB, sm_ag)):
+            if k == 0:
+                pl.when(peer != 0)(functools.partial(chan(k).wait_send, src.at[:size, :], peer))
+            elif k == 1:
+                pl.when(mc != 0)(functools.partial(chan(k).wait_send, src.at[:size, :], peer))
+            else:
+                chan(k).wait_send(src.at[:size, :], peer)
+    for k, src in ((0, dw_send), (1, dw_ag)):
         for peer in seq(k).peers():
-            seq(k).wait_send(src.at[:size, :], peer)
+            seq(k).wait_send(src.at[:RB, :], peer)
     for peer in states(2).peers():
         states(2).wait_send(tot, peer)
     for d in range(1, NS):
@@ -562,6 +625,27 @@
     @pl.when(ms > 0)
     def _():
         halo_copy(halo_a, halo_a, 1, before).wait_send()
+
+    for p in range(2):
+        at = pl.ds(pl.multiple_of(ms * RB + p * PB, PB), PB)
+        xl_ag[at, :] = collect(seq(2 + p), xl_rs.at[p], xl_f[at, :]).astype(BF16)
+        for peer in seq(5 + p).peers():
+            seq(5 + p).send(piece(xl_ag, ms, p), piece(xl_ag, ms, p), peer)
+    at = pl.ds(pl.multiple_of(ms * SB, SB), SB)
+    sm_ag[at, :] = collect(seq(4), sm_rs, sm_own[at, :]).astype(BF16)
+    spread(seq(7), sm_ag, SB)
+    for copy in leave:
+        copy.wait()
+    for k, size, src in ((2, PB, xl_send), (3, PB, xl_send), (4, SB, sm_send)):
+        for peer in seq(k).peers():
+            seq(k).wait_send(src.at[:size, :], peer)
+    for p in range(2):
+        for peer in seq(5 + p).peers():
+            seq(5 + p).wait_recv(piece(xl_ag, peer, p), peer)
+    arrive(seq(7), sm_ag, SB)
+    for k, size, src in ((5, PB, xl_ag), (6, PB, xl_ag), (7, SB, sm_ag)):
+        for peer in seq(k).peers():
+            seq(k).wait_send(src.at[:size, :], peer)
 
 
 def finish_kernel(dims, xg, zg, dw_sum, xl_sum, sm_sum, xg_o, zg_o, cwg_o, cbg_o, xpg_o, dwg_o, dbg_o, alg_o, dsg_o, dgg_o):
@@ -608,7 +692,8 @@
     scratch = dict(
         x_ref=b16(T, C), z_ref=b16(T, C), g_ref=b16(T, C), cw_ref=f32(4, C), cb_ref=f32(1, C), xw_ref=b16(R + 2 * N, C),
         dw_ref=b16(R, C), db_ref=f32(1, C), al_ref=f32(N, C), ds_ref=f32(1, C), dg_ref=f32(1, R),
-        xpad=f32(T + 8, C), pre_act=f32(T, C), act_slope=f32(T, C), u_bf=b16(T, C), gy=f32(T, C), gz=f32(T, C),
+        xg_v=b16(T, C), zg_v=b16(T, C), dw_ag=b16(R, C), shifts=b16(3 * T, T), shifted=b16(3 * T, C),
+        first_parts=b16(NC, ROWS, W), pre_act=f32(T, C), act_slope=f32(T, C), u_bf=b16(T, C), gy=f32(T, C), gz=f32(T, C),
         part=f32(T, W), send1=b16(T, W), rs1=b16(NC, ROWS, W), ag1=b16(T, W),
         low_own=f32(ROWS, R), inv_own=f32(ROWS, LANES),
         pre_soft=f32(T, C), delta=f32(T, C), drive=f32(T, C), bB=f32(T * N, LANES), cB=f32(T * N, LANES),
@@ -618,15 +703,15 @@
         in_tot=f32(NS, 1, C), carry_f=f32(N, C), carry_b=f32(N, C),
         e_exp=b16(GN, GROUP), m_b=f32(GN, LANES), m_c=f32(GN, LANES), sel_b=b16(LANES, GN), sel_c=b16(LANES, GN),
         dmask=f32(CHUNK * GROUP, GN), back_b=b16(GN, LANES), back_c=b16(GN, LANES),
-        b_diag=b16(T, GN), c_diag=b16(T, GN), b_all=f32(T, GN), c_all=f32(T, GN), adj_all=f32(T, HC), by_all=f32(T, HC),
+        tail32=f32(T, LANES), b_diag=b16(T, GN), c_diag=b16(T, GN), b_all=f32(T, GN), c_all=f32(T, GN), adj_all=f32(T, HC), by_all=f32(T, HC),
         uscan=f32(T, C), pregrad=f32(T, C), prehalf=b16(T, C),
         send2=b16(T, W), rs2=b16(NC, ROWS, W), ag2=b16(T, W),
         dw_f=f32(R, C), dw_send=b16(R, C), dw_rs=b16(NS, R // NS, C),
-        xl_f=f32(W, C), xl_send=b16(R, C), xl_rs=b16(NS, R // NS, C),
+        xl_f=f32(W, C), xl_send=b16(R, C), xl_rs=b16(2, NS, R // NS // 2, C),
         sm_f=f32(SM, C), sm_own=f32(2 * SM, HC), sm_send=b16(2 * SM, HC), sm_rs=b16(NS, 2 * SM // NS, HC),
         halo_x=b16(16, C), halo_a=f32(8, C), apad=f32(T + 8, C),
-        s_in=dma((11,)), s_c=dma((4, NC)), r_c=dma((4, NC)), s_st=dma((3, NS)), r_st=dma((3, NS)),
-        s_sq=dma((6, NS)), r_sq=dma((6, NS)), s_h=dma((2,)), r_h=dma((2,)),
+        s_in=dma((11,)), s_out=dma((3,)), s_c=dma((5, NC)), r_c=dma((5, NC)), s_st=dma((3, NS)), r_st=dma((3, NS)),
+        s_sq=dma((8, NS)), r_sq=dma((8, NS)), s_h=dma((2,)), r_h=dma((2,)),
     )
     S = jax.ShapeDtypeStruct
     vmem = pl.BlockSpec(memory_space=pltpu.VMEM)
@@ -634,7 +719,7 @@
         functools.partial(layer_kernel, dims),
         out_shape=(S((T, C), BF16), S((T, C), BF16), S((R, C), BF16), S((R, C), BF16), S((2 * SM, HC), BF16)),
         in_specs=[pl.BlockSpec(memory_space=pl.ANY)] * 11,
-        out_specs=(vmem,) * 5,
+        out_specs=(pl.BlockSpec(memory_space=pl.ANY),) * 3 + (vmem,) * 2,
         scratch_shapes=list(scratch.values()),
         compiler_params=pltpu.CompilerParams(
             collective_id=0, has_side_effects=True, vmem_limit_bytes=VMEM_BYTES

time: 67.8 us -> 63.3 us (0.934)
  Pallas kernels: 67 us -> 62.5 us
    pallas_call x1, Pallas kernels: 64.6 us -> 60.1 us  [per_device(): pl.pallas_call(functools.partial(layer_kernel, dims), out_shape=(S((T, C)...]
where the time goes in v4:
time: 63.3 us; the launch traced here: 63.1 us
  Pallas kernels  62.5 us (99%)
  between operations  0.65 us (1%)
    pallas_call x1, Pallas kernels, per_device(): pl.pallas_call(functools.partial(layer_kernel, dims), out_shape=(S((T, C)...  60.1 us
    pallas_call x1, Pallas kernels, per_device(): pl.pallas_call(functools.partial(finish_kernel, dims), out_shape=(S((T, C...  2.41 us

profile of v4, /device:TPU:1, one launch (start us, length us, event | category | flops | bytes accessed | tf_op | source)
XLA Modules:
  0.0 63.1 jit_solution(11402724723104244114)
XLA Ops:
  0.6 60.1 %shard_map.186 = (bf16[256,512]{1,0:T(8,128)(2,1)}, bf16[256,512]{1,0:T(8,128)(2,1)}, bf16[256,512]{1,0:T(8,128)(2,1)}, bf16[256,512]{1,0:T(8,128)(2,1)}, bf16[128,256]{1,0:T(8,128)(2,1)}) custom-call(bf16[256,512]{1,0:T(8,128)(2,1)} %refs_0_.1, bf16[256,512]{1,0:T(8,128)(2,1)} %refs_1_.1, bf16[256,512]{1,0:T(8,128)(2,1)} %refs_2_.1, f32[4,512]{1,0:T(4,128)} %refs_3_.1, ...), custom_call_target="tpu_custom_call" | custom-call | tf_op jit(solution)/shard_map/pallas_call | solution.py:718
  60.7 2.4 %shard_map.187 = (bf16[256,512]{1,0:T(8,128)(2,1)}, bf16[256,512]{1,0:T(8,128)(2,1)}, f32[4,512]{1,0:T(4,128)}, f32[1,512]{1,0:T(1,128)}, f32[288,512]{1,0:T(8,1...) custom-call(bf16[256,512]{1,0:T(8,128)(2,1)} %get-tuple-element.25.x, ...), custom_call_target="tpu_custom_call" | custom-call | tf_op jit(solution)/shard_map/pallas_call | solution.py:730

commit v5 on v4

--- a/solution.py
+++ b/solution.py
@@ -16,7 +16,7 @@
 BF16 = jnp.bfloat16
 MESH = pl.DeviceIdType.MESH
 VMEM_BYTES = 60 * 1024 * 1024
-CHUNK = 4
+CHUNK = 16
 
 
 def dot(a, b):
@@ -433,16 +433,21 @@
 
     def states_both(i, carry):
         g, h = carry
-        for k in range(2):
-            k = 2 * i + k
+        for k in range(4):
+            k = 4 * i + k
             c_all[tokens(k), :] = c_sums(0, k)
             g, h = backward_block(0, NB - 1 - k, g), forward_block(1, k, h)
         return g, h
 
     forward_carry()
-    lax.fori_loop(0, NB, functools.partial(forward_block, 0), start_states(0))
+    def states_first(i, h):
+        for k in range(4):
+            h = forward_block(0, 4 * i + k, h)
+        return h
+
+    lax.fori_loop(0, NB // 4, states_first, start_states(0))
     backward_carry()
-    lax.fori_loop(0, NB // 2, states_both, (carry_b[:, HALVES[0]], start_states(1)))
+    lax.fori_loop(0, NB // 4, states_both, (carry_b[:, HALVES[0]], start_states(1)))
     CT = CHUNK * GROUP
 
     def backward_chunk(i, g):

time: 63.3 us -> 61.2 us (0.967)
  Pallas kernels: 62.5 us -> 60.3 us
    pallas_call x1, Pallas kernels: 60.1 us -> 57.9 us  [per_device(): pl.pallas_call(functools.partial(layer_kernel, dims), out_shape=(S((T, C)...]
where the time goes in v5:
time: 61.2 us; the launch traced here: 61 us
  Pallas kernels  60.3 us (99%)
  between operations  0.65 us (1%)
    pallas_call x1, Pallas kernels, per_device(): pl.pallas_call(functools.partial(layer_kernel, dims), out_shape=(S((T, C)...  57.9 us
    pallas_call x1, Pallas kernels, per_device(): pl.pallas_call(functools.partial(finish_kernel, dims), out_shape=(S((T, C...  2.41 us

profile of v5, /device:TPU:1, one launch (start us, length us, event | category | flops | bytes accessed | tf_op | source)
XLA Modules:
  0.0 61.0 jit_solution(13360958635786046525)
XLA Ops:
  0.6 57.9 %shard_map.186 = (bf16[256,512]{1,0:T(8,128)(2,1)}, bf16[256,512]{1,0:T(8,128)(2,1)}, bf16[256,512]{1,0:T(8,128)(2,1)}, bf16[256,512]{1,0:T(8,128)(2,1)}, bf16[128,256]{1,0:T(8,128)(2,1)}) custom-call(bf16[256,512]{1,0:T(8,128)(2,1)} %refs_0_.1, bf16[256,512]{1,0:T(8,128)(2,1)} %refs_1_.1, bf16[256,512]{1,0:T(8,128)(2,1)} %refs_2_.1, f32[4,512]{1,0:T(4,128)} %refs_3_.1, ...), custom_call_target="tpu_custom_call" | custom-call | tf_op jit(solution)/shard_map/pallas_call | solution.py:723
  58.6 2.4 %shard_map.187 = (bf16[256,512]{1,0:T(8,128)(2,1)}, bf16[256,512]{1,0:T(8,128)(2,1)}, f32[4,512]{1,0:T(4,128)}, f32[1,512]{1,0:T(1,128)}, f32[288,512]{1,0:T(8,1...) custom-call(bf16[256,512]{1,0:T(8,128)(2,1)} %get-tuple-element.25.x, ...), custom_call_target="tpu_custom_call" | custom-call | tf_op jit(solution)/shard_map/pallas_call | solution.py:735
